TPU v7x, 128 devices: a whole 4x4x4 slice. The times are simulated.
128 devices in a mesh: qa: 8 (over x, z_hi), qb: 16 (over y, z_lo, core).
Axes of the slice: x: 4, y: 4, z: 4 (z_hi: 2, z_lo: 2; z = z_hi * 2 + z_lo), core: 2. Of those that a mesh axis runs over, the one named last changes fastest.
Arguments:
- amplitudes: float32 [8, 16, 262144], P('qa', 'qb'), may hold values from -6 to 6
- gate_angles: float32 [2, 4, 7], replicated, may hold values from -3.140625 to 3.140625
- pair_masks: int32 [2, 4], replicated, may hold values from 0 to 2097151
- control_qubits: int32 [2, 4], replicated, may hold values from 0 to 24
- final_angles: float32 [4], replicated, may hold values from -3.140625 to 3.140625
Outputs:
- final_state: float32 [8, 16, 262144], P('qa', 'qb')
Inputs may be any that keep to these rules, and one draw needn't show every extreme that they name: `pair_masks`: bit p of a mask selects the p-th pair of the gate's seven qubits; every bit is set in some draws. `control_qubits`: any qubit, inside or outside the gate's own seven; a control on the first qubit itself is a Z on it.
All inputs are finite; a program needn't handle non-finite values.
Results may differ from a plain program's by a relative error of at most 0.00014.
Values sent between devices are 32-bit elements; how exact they have to be, the bound alone decides.
A program may use at most 64 MiB of HBM per device.

v0:
```python
import jax
import jax.numpy as jnp
import numpy as np
from jax import lax
from jax.sharding import PartitionSpec as P

LAYERS = 2


def from_partner(value, axis, stride):
    mask = 2**stride
    pairs = [(source, source ^ mask) for source in range(lax.axis_size(axis))]
    return lax.ppermute(value, axis, pairs)


def pair_lists():
    first_list = []
    second_list = []
    for left in range(7):
        for right in range(left + 1, 7):
            first_list.append(left)
            second_list.append(right)
    return (np.array(first_list, np.int32), np.array(second_list, np.int32))


def joined_gate(angles, mask):
    index = jnp.arange(128, dtype=jnp.int32)
    places = jnp.arange(7, dtype=jnp.int32)
    bits = jnp.right_shift(index[:, None], places[None, :]) & 1
    cosine = jnp.cos(angles * 0.5)
    sine = jnp.sin(angles * 0.5)
    rows = bits[:, None, :]
    cols = bits[None, :, :]
    entry = jnp.where(rows == cols, cosine, jnp.where(rows > cols, sine, -sine))
    kron = jnp.prod(entry, axis=2)
    first_list, second_list = pair_lists()
    chosen = jnp.right_shift(mask, jnp.arange(21, dtype=jnp.int32)) & 1
    parity = jnp.sum(chosen[None, :] * bits[:, first_list] * bits[:, second_list], axis=1)
    sign = 1.0 - 2.0 * (parity % 2).astype(jnp.float32)
    return sign[:, None] * kron


def apply_local(vector, matrix, start, width):
    if start == 0:
        shaped = vector.reshape(-1, 128)
        return jnp.dot(shaped, matrix.T, precision=lax.Precision.HIGHEST).reshape(-1)
    shaped = vector.reshape(2 ** (width - 7 - start), 128, 2**start)
    result = jnp.einsum("ij,ajb->aib", matrix, shaped, precision=lax.Precision.HIGHEST)
    return result.reshape(-1)


def shards(amplitudes, gate_angles, pair_masks, control_qubits, final_angles):
    full_shape = amplitudes.shape
    local_count = full_shape[2]
    width = local_count.bit_length() - 1
    count_qa = lax.axis_size("qa")
    count_qb = lax.axis_size("qb")
    global_bits = count_qa.bit_length() - 1 + (count_qb.bit_length() - 1)
    qb_bits = count_qb.bit_length() - 1
    total = width + global_bits
    low_span = 2 ** (7 - global_bits)
    high_span = 2**global_bits
    columns = local_count // 128
    vector = amplitudes.reshape(local_count)
    device = lax.axis_index("qa") * count_qb + lax.axis_index("qb")
    position = device * local_count + jnp.arange(local_count, dtype=jnp.int32)
    starts = [0, 7, width - 7, total - 7]
    order = np.array(
        [slot % high_span * low_span + slot // high_span for slot in range(128)], np.int32
    )
    for layer in range(LAYERS):
        parity = jnp.zeros((local_count,), jnp.int32)
        for gate in range(4):
            own_bit = jnp.right_shift(position, starts[gate]) & 1
            ctrl_bit = jnp.right_shift(position, control_qubits[layer, gate]) & 1
            parity = parity + own_bit * ctrl_bit
        vector = vector * (1.0 - 2.0 * (parity % 2).astype(jnp.float32))
        for gate in range(3):
            matrix = joined_gate(gate_angles[layer, gate], pair_masks[layer, gate])
            vector = apply_local(vector, matrix, starts[gate], width)
        top_gate = joined_gate(gate_angles[layer, 3], pair_masks[layer, 3])
        arranged = top_gate[order][:, order]
        grouped = vector.reshape(low_span, high_span, columns)
        block = lax.all_to_all(grouped, ("qa", "qb"), split_axis=1, concat_axis=1, tiled=True)
        items = block.shape[2]
        mixed = jnp.dot(arranged, block.reshape(128, items), precision=lax.Precision.HIGHEST)
        vector = lax.all_to_all(
            mixed.reshape(low_span, high_span, items),
            ("qa", "qb"),
            split_axis=1,
            concat_axis=1,
            tiled=True,
        ).reshape(local_count)
    for bit in range(qb_bits):
        partner_amps = from_partner(vector, "qb", bit)
        upper_half = jnp.right_shift(lax.axis_index("qb"), bit) & 1
        cosine = jnp.cos(final_angles[bit] * 0.5)
        sine = jnp.sin(final_angles[bit] * 0.5)
        vector = cosine * vector + jnp.where(upper_half == 1, sine, -sine) * partner_amps
    return vector.reshape(full_shape)


def solution(mesh):
    return jax.shard_map(
        shards,
        mesh=mesh,
        in_specs=(P("qa", "qb", None), P(), P(), P(), P()),
        out_specs=P("qa", "qb", None),
        check_vma=False,
    )
```

profile of v0, /device:TPU:1, one launch (start us, length us, event | category | flops | bytes accessed | tf_op | source)
XLA Modules:
  0.0 214.3 jit_solution(11337157175923746340)
XLA Ops:
  0.0 1.0 cosine_bitcast_fusion.4
  1.0 0.1 fusion.133
  1.2 0.7 copy-done.1
  1.8 0.7 fusion.139
  2.5 0.6 shift-right-arithmetic_and_fusion.10
  3.1 0.6 shift-right-arithmetic_and_fusion.11
  3.7 0.7 shift-right-arithmetic_and_fusion.12
  4.4 0.6 shift-right-arithmetic_and_fusion.5
  5.0 0.6 shift-right-arithmetic_and_fusion.6
  5.6 0.7 shift-right-arithmetic_and_fusion.7
  6.3 0.6 shift-right-arithmetic_and_fusion.8
  6.9 0.6 shift-right-arithmetic_and_fusion.9
  7.6 0.6 copy-done.5
  8.2 0.6 gather_fusion
  8.8 0.6 gather_fusion.1
  9.4 0.7 copy-done.2
  10.0 0.7 fusion.138
  10.7 0.1 multiply_reduce_fusion
  10.8 0.6 fusion.61
  11.5 4.9 %fusion.5 = f32[16,128,128]{1,2,0:T(8,128)S(1)} fusion(f32[16,128,128]{2,1,0:T(8,128)S(1)} %bitcast.119, s32[]{:T(128)} %bitcast.14, s32[]{:T(128)} %bitcast.13, s32[]{:T(128)} %bitcast.12, s32[]{:T(128)} %bitcast.11, s32[]{:T(128)S(6)} %mul.405, f32[128,128]{1,0:T(8,128)S(1)} %get-tuple-element.14, f32[128]{0:T(128)S(1)} %get-tuple-element.67), kind=kOutput, calls=%fused_computation.39 | convolution fusion | flops 413941760 | bytes 2163220 | tf_op jit(solution)/shard_map/dot_general | solution.py:46
  16.4 1.1 convolution_bitcast_fusion.5
  17.5 0.3 copy.68
  17.8 0.2 reshape.288
  18.0 1.8 convolution_bitcast_fusion.3
  19.9 1.9 copy.69
  21.8 11.5 %all-to-all-start = ((f32[1,128,2048]{2,0,1:T(1,128)}), f32[1,128,2048]{2,0,1:T(1,128)S(1)}, u32[]{:S(2)}, u32[]{:S(2)}) async-start(f32[1,128,2048]{2,0,1:T(1,128)} %copy.69), calls=%async_computation | async-start | bytes 2097152 | tf_op jit(solution)/shard_map/all_to_all | solution.py:84
  33.3 0.2 fusion.55
  33.6 0.1 broadcast_multiply_fusion
  33.7 0.6 gather_fusion.4
  34.3 0.1 copy.66
  34.4 0.6 gather_fusion.5
  35.1 17.5 %all-to-all-done = f32[1,128,2048]{2,0,1:T(1,128)S(1)} async-done(((f32[1,128,2048]{2,0,1:T(1,128)}), f32[1,128,2048]{2,0,1:T(1,128)S(1)}, u32[]{:S(2)}, u32[]{:S(2)}) %all-to-all-start) | async-done | bytes 1048608 | tf_op jit(solution)/shard_map/all_to_all | solution.py:84
  52.6 1.3 convolution_bitcast_fusion.2
  53.9 2.0 copy.70
  55.9 3.8 %all-to-all-start.1 = ((f32[1,128,2048]{2,0,1:T(1,128)}), f32[1,128,2048]{2,0,1:T(1,128)S(1)}, u32[]{:S(2)}, u32[]{:S(2)}) async-start(f32[1,128,2048]{2,0,1:T(1,128)} %copy.70), calls=%async_computation.1 | async-start | bytes 2097152 | tf_op jit(solution)/shard_map/all_to_all | solution.py:87
  59.8 19.4 %all-to-all-done.1 = f32[1,128,2048]{2,0,1:T(1,128)S(1)} async-done(((f32[1,128,2048]{2,0,1:T(1,128)}), f32[1,128,2048]{2,0,1:T(1,128)S(1)}, u32[]{:S(2)}, u32[]{:S(2)}) %all-to-all-start.1) | async-done | bytes 1048608 | tf_op jit(solution)/shard_map/all_to_all | solution.py:87
  79.3 4.8 %fusion.12 = f32[16,128,128]{1,2,0:T(8,128)S(1)} fusion(f32[16,128,128]{2,1,0:T(8,128)S(1)} %bitcast.118, s32[]{:T(128)} %bitcast.34, s32[]{:T(128)} %bitcast.33, s32[]{:T(128)} %bitcast.32, s32[]{:T(128)} %bitcast.31, s32[]{:T(128)S(6)} %mul.405, f32[128,128]{1,0:T(8,128)S(1)} %get-tuple-element.16, f32[128]{0:T(128)S(1)} %get-tuple-element.71), kind=kOutput, calls=%fused_computation.45 | convolution fusion | flops 413941760 | bytes 2163220 | tf_op jit(solution)/shard_map/dot_general | solution.py:46
  84.1 1.1 convolution_bitcast_fusion.4
  85.1 0.3 copy.72
  85.5 0.2 reshape.292
  85.7 1.8 convolution_bitcast_fusion.1
  87.5 1.9 copy.73
  89.4 3.8 %all-to-all-start.2 = ((f32[1,128,2048]{2,0,1:T(1,128)}), f32[1,128,2048]{2,0,1:T(1,128)S(1)}, u32[]{:S(2)}, u32[]{:S(2)}) async-start(f32[1,128,2048]{2,0,1:T(1,128)} %copy.73), calls=%async_computation.2 | async-start | bytes 2097152 | tf_op jit(solution)/shard_map/all_to_all | solution.py:84
  93.2 0.6 gather_fusion.2
  93.9 0.1 copy.65
  94.0 0.6 gather_fusion.3
  94.6 18.1 %all-to-all-done.2 = f32[1,128,2048]{2,0,1:T(1,128)S(1)} async-done(((f32[1,128,2048]{2,0,1:T(1,128)}), f32[1,128,2048]{2,0,1:T(1,128)S(1)}, u32[]{:S(2)}, u32[]{:S(2)}) %all-to-all-start.2) | async-done | bytes 1048608 | tf_op jit(solution)/shard_map/all_to_all | solution.py:84
  112.7 1.3 convolution_bitcast_fusion
  114.0 1.1 copy.74
  115.1 23.0 %all_to_all.20 = f32[1,128,2048]{2,0,1:T(1,128)S(1)} all-to-all(f32[1,128,2048]{2,0,1:T(1,128)S(1)} %copy.74), channel_id=1, replica_groups=mesh['qa'=8,'qb'=16] {'qa','qb'}, dimensions={1} | all-to-all | bytes 2097152 | tf_op jit(solution)/shard_map/all_to_all | solution.py:87
  138.0 0.4 collective-permute-start
  138.4 0.3 copy-done.3
  138.7 0.7 fusion.140
  140.2 0.6 collective-permute-done
  140.7 0.1 multiply_add_fusion.3
  140.8 0.7 collective-permute-start.1
  142.3 23.0 %collective-permute-done.1 = f32[262144]{0:T(1024)S(1)} collective-permute-done((f32[262144]{0:T(1024)S(1)}, f32[262144]{0:T(1024)S(1)}, u32[]{:S(2)}, u32[]{:S(2)}) %collective-permute-start.1) | collective-permute-done | bytes 1048608 | tf_op jit(solution)/shard_map/ppermute | solution.py:13
  165.3 0.1 multiply_add_fusion.2
  165.4 0.5 collective-permute-start.2
  166.8 22.2 %collective-permute-done.2 = f32[262144]{0:T(1024)S(1)} collective-permute-done((f32[262144]{0:T(1024)S(1)}, f32[262144]{0:T(1024)S(1)}, u32[]{:S(2)}, u32[]{:S(2)}) %collective-permute-start.2) | collective-permute-done | bytes 1048608 | tf_op jit(solution)/shard_map/ppermute | solution.py:13
  188.9 0.1 multiply_add_fusion.1
  189.1 1.7 collective-permute-start.3
  191.5 21.6 %collective-permute-done.3 = f32[262144]{0:T(1024)S(1)} collective-permute-done((f32[262144]{0:T(1024)S(1)}, f32[262144]{0:T(1024)S(1)}, u32[]{:S(2)}, u32[]{:S(2)}) %collective-permute-start.3) | collective-permute-done | bytes 1048608 | tf_op jit(solution)/shard_map/ppermute | solution.py:13
  213.2 1.1 multiply_add_fusion
  (20 shorter events, 0.1 us)
Async XLA Ops:
  0.0 1.0 copy-start
  1.1 0.7 copy-start.1
  6.9 0.7 copy-start.4
  7.5 0.7 copy-start.5
  7.6 3.9 %copy-start.6 = (f32[1,1,262144]{2,1,0:T(1,128)S(1)}, f32[1,1,262144]{2,1,0:T(1,128)}, u32[]{:S(2)}) copy-start(f32[1,1,262144]{2,1,0:T(1,128)} %param.42) | copy-start | bytes 3145732
  9.3 0.7 copy-start.2
  21.8 30.8 %all-to-all-start = ((f32[1,128,2048]{2,0,1:T(1,128)}), f32[1,128,2048]{2,0,1:T(1,128)S(1)}, u32[]{:S(2)}, u32[]{:S(2)}) async-start(f32[1,128,2048]{2,0,1:T(1,128)} %copy.69), calls=%async_computation | async-start | bytes 2097152 | tf_op jit(solution)/shard_map/all_to_all | solution.py:84
  55.9 23.3 %all-to-all-start.1 = ((f32[1,128,2048]{2,0,1:T(1,128)}), f32[1,128,2048]{2,0,1:T(1,128)S(1)}, u32[]{:S(2)}, u32[]{:S(2)}) async-start(f32[1,128,2048]{2,0,1:T(1,128)} %copy.70), calls=%async_computation.1 | async-start | bytes 2097152 | tf_op jit(solution)/shard_map/all_to_all | solution.py:87
  89.4 23.3 %all-to-all-start.2 = ((f32[1,128,2048]{2,0,1:T(1,128)}), f32[1,128,2048]{2,0,1:T(1,128)S(1)}, u32[]{:S(2)}, u32[]{:S(2)}) async-start(f32[1,128,2048]{2,0,1:T(1,128)} %copy.73), calls=%async_computation.2 | async-start | bytes 2097152 | tf_op jit(solution)/shard_map/all_to_all | solution.py:84
  138.0 0.7 copy-start.3
  138.0 2.7 %collective-permute-start = (f32[262144]{0:T(1024)S(1)}, f32[262144]{0:T(1024)S(1)}, u32[]{:S(2)}, u32[]{:S(2)}) collective-permute-start(f32[262144]{0:T(1024)S(1)} %bitcast.116), channel_id=1, source_target_pairs={{0,1},{1,0},{2,3},{3,2},{4,5},{5,4},{6,7},{7,6},{8,9},{9,8},{10,11... | collective-permute-start | bytes 3145736 | tf_op jit(solution)/shard_map/ppermute | solution.py:13
  140.8 24.5 %collective-permute-start.1 = (f32[262144]{0:T(1024)S(1)}, f32[262144]{0:T(1024)S(1)}, u32[]{:S(2)}, u32[]{:S(2)}) collective-permute-start(f32[262144]{0:T(1024)S(1)} %multiply_add_fusion.3), channel_id=1, source_target_pairs={{0,2},{1,3},{2,0},{3,1},{4,6},{5,7},{6,4},{7,5},{8,10},{9,11},{10,... | collective-permute-start | bytes 3145736 | tf_op jit(solution)/shard_map/ppermute | solution.py:13
  165.4 23.5 %collective-permute-start.2 = (f32[262144]{0:T(1024)S(1)}, f32[262144]{0:T(1024)S(1)}, u32[]{:S(2)}, u32[]{:S(2)}) collective-permute-start(f32[262144]{0:T(1024)S(1)} %multiply_add_fusion.2), channel_id=1, source_target_pairs={{0,4},{1,5},{2,6},{3,7},{4,0},{5,1},{6,2},{7,3},{8,12},{9,13},{10,... | collective-permute-start | bytes 3145736 | tf_op jit(solution)/shard_map/ppermute | solution.py:13
  189.1 24.1 %collective-permute-start.3 = (f32[262144]{0:T(1024)S(1)}, f32[262144]{0:T(1024)S(1)}, u32[]{:S(2)}, u32[]{:S(2)}) collective-permute-start(f32[262144]{0:T(1024)S(1)} %multiply_add_fusion.1), channel_id=1, source_target_pairs={{0,8},{1,9},{2,10},{3,11},{4,12},{5,13},{6,14},{7,15},{8,0},{9,1},... | collective-permute-start | bytes 3145736 | tf_op jit(solution)/shard_map/ppermute | solution.py:13
where the time goes:
time: 216 us; the launch traced here: 214 us
  waiting for transfers between devices  122 us (56%)
  blocking collectives  23 us (11%)
  starting transfers between devices  22.4 us (10%)
  matrix products  18.1 us (8%)
  local copies, waits for them, and re-layouts  16 us (7%)
  other arithmetic  8.67 us (4%)
  between operations  3.57 us (2%)
    ppermute x4, waiting for transfers between devices, from_partner(): return lax.ppermute(value, axis, pairs)  67.4 us
    all_to_all x2, waiting for transfers between devices, shards(): lax.all_to_all(grouped, ('qa', 'qb'), split_axis=1, concat_axis=1, tiled=...  35.6 us
    all_to_all x1, blocking collectives, shards(): lax.all_to_all(mixed.reshape(low_span, high_span, items), ('qa', 'qb'), s...  23 us
    all_to_all x1, waiting for transfers between devices, shards(): lax.all_to_all(mixed.reshape(low_span, high_span, items), ('qa', 'qb'), s...  19.4 us
    all_to_all x2, starting transfers between devices, shards(): lax.all_to_all(grouped, ('qa', 'qb'), split_axis=1, concat_axis=1, tiled=...  15.3 us
    dot_general x2, matrix products, apply_local(): jnp.dot(shaped, matrix.T, precision=lax.Precision.HIGHEST).reshape(-1)  9.75 us
    dot_general x4, matrix products, apply_local(): jnp.einsum('ij,ajb->aib', matrix, shaped, precision=lax.Precision.HIGHEST)  5.81 us
    and x8, other arithmetic, joined_gate(): chosen = jnp.right_shift(mask, jnp.arange(21, dtype=jnp.int32)) & 1  4.98 us
  transfers between devices with their start and end apart: 7, of which 7 were waited for; matrix products, arithmetic and copies ran while one was open for 2% of the time, Pallas kernels for 0%

commit v1 on v0

v1 whole, which is shorter than its diff:
```python
import functools
import jax
import jax.numpy as jnp
import numpy as np
from jax import lax
from jax.sharding import PartitionSpec as P
from jax.experimental import pallas as pl
from jax.experimental.pallas import tpu as pltpu

MESH = pl.DeviceIdType.MESH
HI = lax.Precision.HIGHEST


def pair_lists():
    first_list = []
    second_list = []
    for left in range(7):
        for right in range(left + 1, 7):
            first_list.append(left)
            second_list.append(right)
    return (np.array(first_list, np.int32), np.array(second_list, np.int32))


def joined_gate(angles, mask):
    index = jnp.arange(128, dtype=jnp.int32)
    places = jnp.arange(7, dtype=jnp.int32)
    bits = jnp.right_shift(index[:, None], places[None, :]) & 1
    cosine = jnp.cos(angles * 0.5)
    sine = jnp.sin(angles * 0.5)
    rows = bits[:, None, :]
    cols = bits[None, :, :]
    entry = jnp.where(rows == cols, cosine, jnp.where(rows > cols, sine, -sine))
    kron = jnp.prod(entry, axis=2)
    first_list, second_list = pair_lists()
    chosen = jnp.right_shift(mask, jnp.arange(21, dtype=jnp.int32)) & 1
    parity = jnp.sum(chosen[None, :] * bits[:, first_list] * bits[:, second_list], axis=1)
    sign = 1.0 - 2.0 * (parity % 2).astype(jnp.float32)
    return sign[:, None] * kron


def closing(angles):
    index = jnp.arange(128, dtype=jnp.int32)
    places = jnp.arange(4, dtype=jnp.int32)
    bits = jnp.right_shift(index[:, None], places[None, :]) & 1
    cosine = jnp.cos(angles * 0.5)
    sine = jnp.sin(angles * 0.5)
    rows = bits[:, None, :]
    cols = bits[None, :, :]
    entry = jnp.where(rows == cols, cosine, jnp.where(rows > cols, sine, -sine))
    same = (index[:, None] // 16 == index[None, :] // 16).astype(jnp.float32)
    return jnp.prod(entry, axis=2) * same


def a2a_kernel(x_ref, o_ref, send_sem, recv_sem, own_sem):
    qa = lax.axis_index("qa")
    qb = lax.axis_index("qb")
    me = qa * 16 + qb
    x, zh, y, zl, c = qa // 2, qa % 2, qb // 4, (qb // 2) % 2, qb % 2
    z = zh * 2 + zl

    def target(step):
        tc = (c + step % 2) % 2
        tz = (z + (step // 2) % 4) % 4
        ty = (y + (step // 8) % 4) % 4
        tx = (x + step // 32) % 4
        ta = tx * 2 + tz // 2
        tb = ty * 4 + (tz % 2) * 2 + tc
        return ta, tb, ta * 16 + tb

    barrier = pltpu.get_barrier_semaphore()

    def greet(step, carry):
        ta, tb, _ = target(step)
        pl.semaphore_signal(barrier, inc=1, device_id=(ta, tb), device_id_type=MESH)
        return carry

    lax.fori_loop(1, 128, greet, 0)
    own = pltpu.make_async_copy(x_ref.at[me], o_ref.at[me], own_sem)
    own.start()
    pl.semaphore_wait(barrier, 127)

    def send(step, carry):
        ta, tb, index = target((step * 37) % 128)
        pltpu.make_async_remote_copy(
            x_ref.at[index], o_ref.at[me], send_sem, recv_sem,
            device_id=(ta, tb), device_id_type=MESH,
        ).start()
        return carry

    lax.fori_loop(1, 128, send, 0)
    own.wait()
    block = x_ref.at[pl.ds(0, 127)]
    pltpu.make_async_copy(block, block, send_sem).wait()
    pltpu.make_async_copy(block, block, recv_sem).wait()


def exchange(block):
    return pl.pallas_call(
        a2a_kernel,
        out_shape=jax.ShapeDtypeStruct((128, 16, 128), jnp.float32),
        in_specs=[pl.BlockSpec(memory_space=pltpu.VMEM)],
        out_specs=pl.BlockSpec(memory_space=pltpu.VMEM),
        scratch_shapes=[pltpu.SemaphoreType.DMA] * 3,
        compiler_params=pltpu.CompilerParams(collective_id=0, has_side_effects=True),
        name="exchange",
    )(block)


def shards(amplitudes, gate_angles, pair_masks, control_qubits, final_angles):
    device = lax.axis_index("qa") * 16 + lax.axis_index("qb")
    starts = [0, 7, 11, 18]

    def signs(layer, position):
        parity = jnp.zeros(position.shape, jnp.int32)
        for gate in range(4):
            own_bit = jnp.right_shift(position, starts[gate]) & 1
            ctrl_bit = jnp.right_shift(position, control_qubits[layer, gate]) & 1
            parity = parity + own_bit * ctrl_bit
        return 1.0 - 2.0 * (parity % 2).astype(jnp.float32)

    gates = [[joined_gate(gate_angles[l, g], pair_masks[l, g]) for g in range(4)] for l in range(2)]
    low = jnp.arange(2048, dtype=jnp.int32).reshape(16, 128)
    slot = jnp.arange(128, dtype=jnp.int32)[:, None, None]
    vector = amplitudes.reshape(128, 16, 128)
    vector = vector * signs(0, device * 262144 + slot * 2048 + low)
    def local(layer, vector):
        mixed = jnp.einsum("ij,ajb->aib", gates[layer][1], vector.reshape(16, 128, 128), precision=HI)
        return jnp.dot(gates[layer][2], mixed.reshape(128, 2048), precision=HI).reshape(128, 16, 128)

    vector = exchange(local(0, vector))
    vector = jnp.dot(gates[0][3], vector.reshape(128, 2048), precision=HI).reshape(2048, 128)
    vector = jnp.dot(vector, gates[0][0].T, precision=HI)
    vector = vector.reshape(128, 16, 128) * signs(1, slot * 262144 + device * 2048 + low)
    top = jnp.dot(closing(final_angles), gates[1][3], precision=HI)
    vector = jnp.dot(top, vector.reshape(128, 2048), precision=HI).reshape(2048, 128)
    vector = jnp.dot(vector, gates[1][0].T, precision=HI)
    vector = exchange(vector.reshape(128, 16, 128))
    return local(1, vector).reshape(amplitudes.shape)


def solution(mesh):
    return jax.shard_map(
        shards,
        mesh=mesh,
        in_specs=(P("qa", "qb", None), P(), P(), P(), P()),
        out_specs=P("qa", "qb", None),
        check_vma=False,
    )
```

time: 216 us -> 98.9 us (0.46)
  waiting for transfers between devices: 122 us -> 0 us
  Pallas kernels: 0 us -> 57.6 us
  blocking collectives: 23 us -> 0 us
  starting transfers between devices: 22.4 us -> 0 us
  local copies, waits for them, and re-layouts: 16 us -> 12.5 us
  between operations: 3.57 us -> 0.36 us
  other arithmetic: 8.67 us -> 11.1 us
    ppermute x4 -> x0, waiting for transfers between devices: 67.4 us -> none  [from_partner(): return lax.ppermute(value, axis, pairs)]
    pallas_call x0 -> x2, Pallas kernels: none -> 57.6 us  [exchange(): pl.pallas_call(a2a_kernel, out_shape=jax.ShapeDtypeStruct((128, 16, 128),...]
    all_to_all x3 -> x0, waiting for transfers between devices: 55.1 us -> none  [the longest x2 35.6 us: shards(): lax.all_to_all(grouped, ('qa', 'qb'), split_axis=1, concat_axis=1, tiled=...]
    all_to_all x1 -> x0, blocking collectives: 23 us -> none  [shards(): lax.all_to_all(mixed.reshape(low_span, high_span, items), ('qa', 'qb'), s...]
    all_to_all x3 -> x0, starting transfers between devices: 19.2 us -> none  [the longest x2 15.3 us: shards(): lax.all_to_all(grouped, ('qa', 'qb'), split_axis=1, concat_axis=1, tiled=...]
    transpose x4 -> x2, local copies, waits for them, and re-layouts: 4.45 us -> 0.66 us  [local(): jnp.einsum('ij,ajb->aib', gates[layer][1], vector.reshape(16, 128, 128),...]
    rem x0 -> x1, other arithmetic: none -> 3.77 us  [signs(): return 1.0 - 2.0 * (parity % 2).astype(jnp.float32)]
    ppermute x4 -> x0, starting transfers between devices: 3.26 us -> none  [from_partner(): return lax.ppermute(value, axis, pairs)]
  transfers between devices with their start and end apart: 7 -> 0, of which waited for: 7 -> 0; matrix products, arithmetic and copies ran while one was open for 2% -> 0% of each run, Pallas kernels for 0% -> 0%
where the time goes in v1:
time: 98.9 us; the launch traced here: 98.4 us
  Pallas kernels  57.6 us (58%)
  matrix products  16.8 us (17%)
  local copies, waits for them, and re-layouts  12.5 us (13%)
  other arithmetic  11.1 us (11%)
    pallas_call x2, Pallas kernels, exchange(): pl.pallas_call(a2a_kernel, out_shape=jax.ShapeDtypeStruct((128, 16, 128),...  57.6 us
    dot_general x2, matrix products, local(): jnp.einsum('ij,ajb->aib', gates[layer][1], vector.reshape(16, 128, 128),...  5.07 us
    and x8, other arithmetic, joined_gate(): chosen = jnp.right_shift(mask, jnp.arange(21, dtype=jnp.int32)) & 1  4.98 us
    dot_general x1, matrix products, shards(): vector = jnp.dot(vector, gates[0][0].T, precision=HI)  4.74 us
    unnamed x15, local copies, waits for them, and re-layouts  4.35 us
    rem x1, other arithmetic, signs(): return 1.0 - 2.0 * (parity % 2).astype(jnp.float32)  3.77 us
    dot_general x1, matrix products, shards(): vector = jnp.dot(vector, gates[1][0].T, precision=HI)  2.5 us
    another operation x1, local copies, waits for them, and re-layouts, shards(): return local(1, vector).reshape(amplitudes.shape)  2.22 us

profile of v1, /device:TPU:1, one launch (start us, length us, event | category | flops | bytes accessed | tf_op | source)
XLA Modules:
  0.0 98.4 jit_solution(14496690205161020193)
XLA Ops:
  0.0 1.0 %cosine_bitcast_fusion.3 = (f32[7]{0:T(128)S(1)}, f32[7]{0:T(128)S(1)}, f32[7]{0:T(128)S(1)}, f32[7]{0:T(128)S(1)}, f32[7]{0:T(128)S(1)}, /*index=5*/f32[7]{0:T(...) fusion(f32[2,4,7]{2,1,0:T(4,128)} %param.38), kind=kLoop, calls=%fused_computation.222 | loop fusion | flops 56 | bytes 672 | tf_op jit(solution)/shard_map/cos | solution.py:28
  1.0 0.0 copy-start.1
  1.0 0.7 copy-done.1
  1.7 0.1 fusion.138
  1.8 0.6 fusion.58
  2.5 0.0 copy-start.2
  2.5 0.7 copy-done.2
  3.2 0.7 fusion.143
  3.8 0.6 shift-right-arithmetic_and_fusion.2
  4.5 0.6 shift-right-arithmetic_and_fusion.3
  5.0 0.7 shift-right-arithmetic_and_fusion.4
  5.7 0.6 shift-right-arithmetic_and_fusion.5
  6.3 0.6 shift-right-arithmetic_and_fusion.6
  7.0 0.6 shift-right-arithmetic_and_fusion.7
  7.6 0.6 shift-right-arithmetic_and_fusion.8
  8.2 0.0 copy-start.4
  8.2 0.6 shift-right-arithmetic_and_fusion.9
  8.9 0.0 copy-done.4
  8.9 0.0 copy-start.5
  8.9 0.6 gather_fusion
  9.5 0.1 copy-done.5
  9.6 0.6 gather_fusion.1
  10.1 0.1 multiply_reduce_fusion.7
  10.3 0.0 copy-start.3
  10.3 0.7 copy-done.3
  10.9 0.7 fusion.142
  11.6 0.1 add.238
  11.7 0.1 add.239
  11.8 0.1 add.241.clone
  11.9 0.0 copy-start
  11.9 3.8 %negate_select_fusion.2 = s32[16,128,128]{2,1,0:T(8,128)S(1)} fusion(s32[]{:T(128)} %bitcast.20, s32[]{:T(128)} %bitcast.19, s32[]{:T(128)} %bitcast.18, s32[]{:T(128)} %bitcast.17, s32[16,128]{1,0:T(8,128)S(1)} %add.239, s32[16,128,128]{2,1,0:T(8,128)S(1)} %bitcast.179), kind=kLoop, calls=%fused_computation.14 | loop fusion | flops 7864320 | bytes 2105360 | tf_op jit(solution)/shard_map/jit(remainder)/rem | solution.py:119
  15.7 0.0 copy-done
  15.7 2.0 %convolution_bitcast_fusion.1 = f32[16,128,128]{1,2,0:T(8,128)S(1)} fusion(f32[16,128,128]{2,1,0:T(8,128)S(1)} %bitcast.185, s32[16,128,128]{2,1,0:T(8,128)S(1)} %negate_select_fusion.2, f32[128,128]{1,0:T(8,128)S(1)} %get-tuple-element.18, f32[128]{0:T(128)S(1)} %get-tuple-element.68), kind=kOutput, calls=%fused_computation.19 | convolution fusion | flops 405028864 | bytes 3211776 | tf_op jit(solution)/shard_map/ij,ajb->aib/dot_general | solution.py:127
  17.7 0.3 copy.56
  18.0 0.2 reshape.386
  18.2 0.3 copy.67
  18.6 0.2 fusion.61
  18.8 1.1 %fusion.70 = f32[128,16,128]{2,0,1:T(8,128)S(1)} fusion(f32[16,128,128]{2,1,0:T(8,128)S(1)} %bitcast.178, f32[128,128]{1,0:T(8,128)S(1)} %get-tuple-element.19, f32[128]{0:T(128)S(1)} %get-tuple-element.67), kind=kOutput, calls=%fused_computation.108 | convolution fusion | flops 402669568 | bytes 2163200 | tf_op jit(solution)/shard_map/dot_general | solution.py:128
  19.9 1.6 %copy.58.x_ref = f32[128,16,128]{2,1,0:T(8,128)} copy(f32[128,16,128]{2,0,1:T(8,128)S(1)} %fusion.70) | data formatting | bytes 2097152 | tf_op jit(solution)/shard_map/dot_general | solution.py:128
  21.4 31.4 %exchange.2 = f32[128,16,128]{2,1,0:T(8,128)} custom-call(f32[128,16,128]{2,1,0:T(8,128)} %copy.58.x_ref), custom_call_target="tpu_custom_call" | custom-call | tf_op jit(solution)/shard_map/exchange/pallas_call | solution.py:98
  52.8 1.6 %copy.73 = f32[16,8,16,128]{3,1,2,0:T(8,128)S(1)} copy(f32[16,8,16,128]{3,2,1,0:T(8,128)} %bitcast.183) | data formatting | bytes 2097152
  54.4 0.3 copy.59
  54.7 1.1 %fusion.72 = f32[128,16,128]{2,0,1:T(8,128)S(1)} fusion(f32[16,128,128]{2,1,0:T(8,128)S(1)} %bitcast.180, f32[128,128]{1,0:T(8,128)S(1)} %get-tuple-element.14, f32[128]{0:T(128)S(1)} %get-tuple-element.66), kind=kOutput, calls=%fused_computation.110 | convolution fusion | flops 402669568 | bytes 2163200 | tf_op jit(solution)/shard_map/dot_general | solution.py:131
  55.8 4.7 %fusion = f32[16,128,128]{2,1,0:T(8,128)S(1)} fusion(f32[128,16,128]{2,0,1:T(8,128)S(1)} %fusion.72, s32[]{:T(128)} %bitcast.37, s32[]{:T(128)} %bitcast.36, s32[]{:T(128)} %bitcast.35, s32[]{:T(128)} %bitcast.34, s32[128]{0:T(128)S(1)} %multiply_add_fusion.2, s32[16,128]{1,0:T(8,128)S(1)} %multiply_add_fusion, f32[128,128]{1,0:T(8,128)S(1)} %get-tuple-element.17, ...), kind=kOutput, calls=%fused_computation.18 | convolution fusion | flops 412893184 | bytes 2171920 | tf_op jit(solution)/shard_map/dot_general | solution.py:132
  60.6 0.0 copy-start.6
  60.6 0.6 copy-done.6
  61.3 0.1 select_reduce_fusion
  61.4 0.3 convolution_bitcast_fusion.2
  61.7 1.0 %fusion.144 = f32[128,16,128]{2,0,1:T(8,128)S(1)} fusion(f32[128,128,1]{1,0,2:T(8,128)S(1)} %convolution_bitcast_fusion.2, f32[16,128,128]{2,1,0:T(8,128)S(1)} %fusion), kind=kOutput, calls=%fused_computation.259 | convolution fusion | flops 402653184 | bytes 2162688 | tf_op jit(solution)/shard_map/dot_general | solution.py:135
  62.8 2.5 %fusion.49.x_ref = f32[128,16,128]{2,1,0:T(8,128)} fusion(f32[128,16,128]{2,0,1:T(8,128)S(1)} %fusion.144, f32[128,128]{1,0:T(8,128)S(1)} %get-tuple-element.16, f32[128]{0:T(128)S(1)} %get-tuple-element.70), kind=kOutput, calls=%fused_computation.86 | convolution fusion | flops 402669568 | bytes 2163200 | tf_op jit(solution)/shard_map/dot_general | solution.py:136
  65.3 26.2 %exchange.3 = f32[128,16,128]{2,1,0:T(8,128)} custom-call(f32[128,16,128]{2,1,0:T(8,128)} %fusion.49.x_ref), custom_call_target="tpu_custom_call" | custom-call | tf_op jit(solution)/shard_map/exchange/pallas_call | solution.py:98
  91.5 3.1 %convolution_bitcast_fusion = f32[16,128,128]{1,2,0:T(8,128)S(1)} fusion(f32[16,128,128]{2,1,0:T(8,128)} %bitcast.181, f32[128,128]{1,0:T(8,128)S(1)} %get-tuple-element.15, f32[128]{0:T(128)S(1)} %get-tuple-element.71), kind=kOutput, calls=%fused_computation.16 | convolution fusion | flops 402669568 | bytes 2163200 | tf_op jit(solution)/shard_map/ij,ajb->aib/dot_general | solution.py:127
  94.6 0.3 copy.62
  94.9 0.2 reshape.390
  95.1 1.0 %fusion.82 = f32[128,2048]{1,0:T(8,128)S(1)} fusion(f32[128,2048]{1,0:T(8,128)S(1)} %reshape.390, f32[128,128]{1,0:T(8,128)S(1)} %get-tuple-element.13, f32[128]{0:T(128)S(1)} %get-tuple-element.64), kind=kOutput, calls=%fused_computation.120 | convolution fusion | flops 402669568 | bytes 2163200 | tf_op jit(solution)/shard_map/dot_general | solution.py:128
  96.2 2.2 %reshape_reshape.3 = f32[1,1,262144]{2,1,0:T(1,128)} reshape(f32[128,2048]{1,0:T(8,128)S(1)} %fusion.82) | data formatting | bytes 2097152 | tf_op jit(solution)/shard_map/reshape;reshape | solution.py:138
  (13 shorter events, 0.1 us)
Async XLA Ops:
  1.0 0.7 copy-start.1
  2.5 0.7 copy-start.2
  8.2 0.7 copy-start.4
  8.9 0.7 copy-start.5
  10.3 0.7 copy-start.3
  11.9 3.8 %copy-start = (f32[1,1,262144]{2,1,0:T(1,128)S(1)}, f32[1,1,262144]{2,1,0:T(1,128)}, u32[]{:S(2)}) copy-start(f32[1,1,262144]{2,1,0:T(1,128)} %param.37) | copy-start | bytes 3145732
  60.6 0.7 copy-start.6

commit v2 on v0

v2 whole, which is shorter than its diff:
```python
import jax
import jax.numpy as jnp
from jax import lax
from jax.sharding import PartitionSpec as P
from jax.experimental import pallas as pl
from jax.experimental.pallas import tpu as pltpu

F32 = jnp.float32
BF16 = jnp.bfloat16
NATURAL = (0, 1, 2, 3, 4, 5, 6)
MOVED = (6, 3, 4, 5, 0, 1, 2)
STARTS = (0, 7, 11, 18)


def iota(shape, dim):
    return lax.broadcasted_iota(jnp.int32, shape, dim)


def halves(value):
    high = value.astype(BF16)
    return high, (value - high.astype(F32)).astype(BF16)


def gate_parity(index, places, mask):
    bits = [index >> places[j] for j in range(7)]
    parity = None
    pair = 0
    for j in range(6):
        inner = None
        for k in range(j + 1, 7):
            term = (mask >> pair) & bits[k]
            inner = term if inner is None else inner ^ term
            pair += 1
        term = inner & bits[j]
        parity = term if parity is None else parity ^ term
    return parity & 1


def kron_rows(cosine, sine, row_places, col_places, flip):
    lane = iota((1, 128), 1)
    zero, one = [], []
    for j in range(7):
        bit = ((lane >> col_places[j]) & 1) == 1
        low, up = (sine[j], -sine[j]) if flip else (-sine[j], sine[j])
        zero.append(jnp.where(bit, low, cosine[j]))
        one.append(jnp.where(bit, cosine[j], up))
    at = [row_places.index(place) for place in range(7)]
    sub = iota((8, 128), 0)
    value = None
    for place in range(3):
        j = at[place]
        factor = jnp.where(((sub >> place) & 1) == 1, one[j], zero[j])
        value = factor if value is None else value * factor
    for place in range(3, 7):
        j = at[place]
        value = jnp.concatenate([value * zero[j], value * one[j]], axis=0)
    return value


def closing_rows(cosine, sine):
    lane = iota((128, 128), 1)
    row = iota((128, 128), 0)
    value = jnp.where((row >> 4) == (lane >> 4), 1.0, 0.0)
    for j in range(4):
        up = (row >> j) & 1
        across = (lane >> j) & 1
        value = value * jnp.where(up == across, cosine[j], jnp.where(up > across, sine[j], -sine[j]))
    return value


def row_gate(left, value):
    high, low = halves(value)
    out = jnp.dot(left, jnp.concatenate([high, low], axis=0), preferred_element_type=F32)
    return out[:128] + out[128:]


def lane_gate(right, value):
    high, low = halves(value)
    out = jnp.dot(jnp.concatenate([high, low], axis=1), right, preferred_element_type=F32)
    return out[:, :128] + out[:, 128:]


def store_row_matrix(ref, slot, matrix):
    high, low = halves(matrix)
    ref[slot] = jnp.concatenate(
        [jnp.concatenate([high, high], axis=1), jnp.concatenate([low, low], axis=1)], axis=0
    )


def store_lane_matrix(ref, slot, matrix):
    high, low = halves(matrix)
    both = jnp.concatenate([high, low], axis=1)
    ref[slot] = jnp.concatenate([both, both], axis=0)


def kernel(
    x_hbm, angles, masks, controls, final, out_hbm,
    x_v, mid, send1, recv1, send2, recv2, signs, row_mats, lane_mats,
    in_sem, own_sem, send_sem, recv_sem,
):
    qa = lax.axis_index("qa")
    qb = lax.axis_index("qb")
    me = qa * 16 + qb
    load = pltpu.make_async_copy(x_hbm, x_v, in_sem)
    load.start()

    x, zh = lax.div(qa, 2), lax.rem(qa, 2)
    y, zl, core = lax.div(qb, 4), lax.rem(lax.div(qb, 2), 2), lax.rem(qb, 2)
    z = zh * 2 + zl
    near = []
    for dz in (2, 1, 3, 0):
        tz = lax.rem(z + dz, 4)
        for dc in (1, 0):
            tc = lax.rem(core + dc, 2)
            near.append(lax.div(tz, 2) * 16 + lax.rem(tz, 2) * 2 + tc)

    def everyone(action):
        def far(step, carry):
            base = lax.rem(x + lax.div(step, 4) + 2, 4) * 32 + lax.rem(y + lax.rem(step, 4) + 2, 4) * 4
            for other in near:
                action(base + other)
            return carry

        lax.fori_loop(0, 10, far, 0)
        lax.fori_loop(11, 16, far, 0)
        for other in near[:7]:
            action(x * 32 + y * 4 + other)

    barrier = pltpu.get_barrier_semaphore()
    everyone(lambda target: pl.semaphore_signal(
        barrier, inc=1, device_id=target, device_id_type=pl.DeviceIdType.LOGICAL))

    lane1 = iota((1, 128), 1)
    mask_lanes = jnp.zeros((1, 128), jnp.int32)
    for layer in range(2):
        for gate in range(4):
            mask_lanes = jnp.where(lane1 == layer * 4 + gate, masks[layer, gate], mask_lanes)
    row = iota((128, 128), 0)
    sign_nat = 1.0 - 2.0 * gate_parity(row, NATURAL, mask_lanes).astype(F32)
    sign_mov = 1.0 - 2.0 * gate_parity(row, MOVED, mask_lanes).astype(F32)
    cos_all = [jnp.cos(angles[layer] * 0.5) for layer in range(2)]
    sin_all = [jnp.sin(angles[layer] * 0.5) for layer in range(2)]

    def splats(table, gate):
        return [jnp.broadcast_to(table[gate:gate + 1, j:j + 1], (1, 128)) for j in range(7)]

    def row_matrix(layer, gate, row_places, col_places):
        value = kron_rows(splats(cos_all[layer], gate), splats(sin_all[layer], gate), row_places, col_places, False)
        sign = sign_nat if row_places is NATURAL else sign_mov
        column = layer * 4 + gate
        return value * sign[:, column:column + 1]

    def lane_matrix(layer):
        value = kron_rows(splats(cos_all[layer], 0), splats(sin_all[layer], 0), NATURAL, NATURAL, True)
        return value * (1.0 - 2.0 * gate_parity(lane1, NATURAL, masks[layer, 0]).astype(F32))

    def parity_at(layer, position):
        parity = None
        for gate in range(4):
            term = (position >> STARTS[gate]) & (position >> controls[layer, gate])
            parity = term if parity is None else parity ^ term
        return parity & 1

    store_row_matrix(row_mats, 0, row_matrix(0, 1, MOVED, NATURAL))
    store_row_matrix(row_mats, 1, row_matrix(0, 2, NATURAL, NATURAL))
    load.wait()

    spot = row * 128 + iota((128, 128), 1) + me * 262144

    def first_gate(pair, carry):
        blocks = []
        for i in range(2):
            a = pair * 2 + i
            value = x_v[pl.ds(pl.multiple_of(a * 128, 128), 128), :]
            blocks.append(jnp.where(parity_at(0, spot + a * 16384) == 1, -value, value))
        out = row_gate(row_mats[0], jnp.concatenate(blocks, axis=1))
        for i in range(2):
            at = pl.multiple_of((pair * 2 + i) * 8, 8)
            mid[:, pl.ds(at, 8), :] = out[:, i * 128:(i + 1) * 128].reshape(16, 8, 128)
        return carry

    lax.fori_loop(0, 8, first_gate, 0)

    def second_gate(pair, carry):
        kk = pair * 2
        out = row_gate(row_mats[1], jnp.concatenate([mid[kk], mid[kk + 1]], axis=1))
        for i in range(2):
            chunk, group = lax.div(kk + i, 8), lax.rem(kk + i, 8)
            part = out[:, i * 128:(i + 1) * 128].reshape(16, 8, 128)
            for a in range(16):
                send1[chunk, pl.ds(pl.multiple_of((a * 8 + group) * 8, 8), 8), :] = part[a]
        return carry

    lax.fori_loop(0, 8, second_gate, 0)
    pl.semaphore_wait(barrier, 127)

    def rows_of(device):
        return pl.ds(pl.multiple_of(device * 8, 8), 8)

    def ship(stage, chunk, source, landing):
        slot = stage * 2 + chunk
        own = pltpu.make_async_copy(
            source.at[chunk, rows_of(me)], landing.at[chunk, rows_of(me)], own_sem.at[slot])
        own.start()
        everyone(lambda target: pltpu.make_async_remote_copy(
            source.at[chunk, rows_of(target)], landing.at[chunk, rows_of(me)],
            send_sem.at[slot], recv_sem.at[slot],
            device_id=target, device_id_type=pl.DeviceIdType.LOGICAL).start())

    def landed(stage, chunk, source, landing):
        slot = stage * 2 + chunk
        pltpu.make_async_copy(
            source.at[chunk, rows_of(me)], landing.at[chunk, rows_of(me)], own_sem.at[slot]).wait()
        others = landing.at[chunk, pl.ds(0, 127 * 8)]
        pltpu.make_async_copy(others, others, recv_sem.at[slot]).wait()

    ship(0, 0, send1, recv1)
    ship(0, 1, send1, recv1)

    store_row_matrix(row_mats, 2, row_matrix(0, 3, NATURAL, NATURAL))
    store_lane_matrix(lane_mats, 0, lane_matrix(0))
    store_lane_matrix(lane_mats, 1, lane_matrix(1))
    final_half = jnp.zeros((1, 128), F32)
    for j in range(4):
        final_half = jnp.where(lane1 == j, final[j] * 0.5, final_half)
    final_cos, final_sin = jnp.cos(final_half), jnp.sin(final_half)
    closing = closing_rows(
        [jnp.broadcast_to(final_cos[:, j:j + 1], (1, 128)) for j in range(4)],
        [jnp.broadcast_to(final_sin[:, j:j + 1], (1, 128)) for j in range(4)])
    store_row_matrix(row_mats, 6, closing)
    top = row_matrix(1, 3, NATURAL, NATURAL)
    store_row_matrix(row_mats, 3, row_gate(row_mats[6], jnp.concatenate([top, top], axis=1))[:, :128])
    store_row_matrix(row_mats, 4, row_matrix(1, 1, MOVED, MOVED))
    store_row_matrix(row_mats, 5, row_matrix(1, 2, NATURAL, NATURAL))
    here = lax.rem(me, 8) * 256 + lax.div(me, 8) * 16384
    device_spot = row * 262144 + iota((128, 128), 1) + here

    def layer_signs(block, carry):
        spots = device_spot + (lax.div(block, 8) * 128 + lax.rem(block, 8) * 2048)
        signs[block] = jnp.where(parity_at(1, spots) == 1, -1.0, 1.0)
        return carry

    lax.fori_loop(0, 16, layer_signs, 0)

    for chunk in range(2):
        landed(0, chunk, send1, recv1)
        for m in range(0, 8, 2):
            value = jnp.concatenate(
                [recv1[chunk, pl.ds(m + i, 128, stride=8), :] for i in range(2)], axis=1)
            value = row_gate(row_mats[2], value)
            value = jnp.concatenate([value[:, :128], value[:, 128:]], axis=0)
            value = lane_gate(lane_mats[0], value)
            block = chunk * 8 + m
            value = value * jnp.concatenate([signs[block], signs[block + 1]], axis=0)
            value = lane_gate(lane_mats[1], value)
            value = jnp.concatenate([value[:128], value[128:]], axis=1)
            value = row_gate(row_mats[3], value)
            for i in range(2):
                send2[chunk, pl.ds(m + i, 128, stride=8), :] = value[:, i * 128:(i + 1) * 128]
        ship(1, chunk, send2, recv2)

    for chunk in range(2):
        landed(1, chunk, send2, recv2)

    def third_gate(pair, carry):
        blocks = []
        for i in range(2):
            rows = pl.ds(pl.multiple_of((pair * 2 + i) * 64, 64), 64)
            blocks.append(jnp.concatenate([recv2[0, rows, :], recv2[1, rows, :]], axis=0))
        out = row_gate(row_mats[4], jnp.concatenate(blocks, axis=1))
        for i in range(2):
            at = pl.multiple_of((pair * 2 + i) * 8, 8)
            mid[:, pl.ds(at, 8), :] = out[:, i * 128:(i + 1) * 128].reshape(16, 8, 128)
        return carry

    lax.fori_loop(0, 8, third_gate, 0)
    for kk in range(0, 16, 2):
        out = row_gate(row_mats[5], jnp.concatenate([mid[kk], mid[kk + 1]], axis=1))
        for i in range(2):
            k = (kk + i) // 8 + 2 * ((kk + i) % 8)
            x_v[pl.ds(k, 128, stride=16), :] = out[:, i * 128:(i + 1) * 128]
    store = pltpu.make_async_copy(x_v, out_hbm, in_sem)
    store.start()
    for slot in range(4):
        source = (send1, send2)[slot // 2]
        others = source.at[slot % 2, pl.ds(0, 127 * 8)]
        pltpu.make_async_copy(others, others, send_sem.at[slot]).wait()
    store.wait()


def shards(amplitudes, gate_angles, pair_masks, control_qubits, final_angles):
    out = pl.pallas_call(
        kernel,
        out_shape=jax.ShapeDtypeStruct((2048, 128), F32),
        in_specs=[
            pl.BlockSpec(memory_space=pl.ANY),
            pl.BlockSpec(memory_space=pltpu.VMEM),
            pl.BlockSpec(memory_space=pltpu.SMEM),
            pl.BlockSpec(memory_space=pltpu.SMEM),
            pl.BlockSpec(memory_space=pltpu.SMEM),
        ],
        out_specs=pl.BlockSpec(memory_space=pl.ANY),
        scratch_shapes=[
            pltpu.VMEM((2048, 128), F32),
            pltpu.VMEM((16, 128, 128), F32),
            pltpu.VMEM((2, 1024, 128), F32),
            pltpu.VMEM((2, 1024, 128), F32),
            pltpu.VMEM((2, 1024, 128), F32),
            pltpu.VMEM((2, 1024, 128), F32),
            pltpu.VMEM((16, 128, 128), F32),
            pltpu.VMEM((7, 256, 256), BF16),
            pltpu.VMEM((2, 256, 256), BF16),
            pltpu.SemaphoreType.DMA,
            pltpu.SemaphoreType.DMA((4,)),
            pltpu.SemaphoreType.DMA((4,)),
            pltpu.SemaphoreType.DMA((4,)),
        ],
        compiler_params=pltpu.CompilerParams(
            collective_id=0, has_side_effects=True, vmem_limit_bytes=24 * 2**20),
        name="layers",
    )(amplitudes.reshape(2048, 128), gate_angles, pair_masks, control_qubits, final_angles)
    return out.reshape(amplitudes.shape)


def solution(mesh):
    return jax.shard_map(
        shards,
        mesh=mesh,
        in_specs=(P("qa", "qb", None), P(), P(), P(), P()),
        out_specs=P("qa", "qb", None),
        check_vma=False,
    )
```

time: 216 us -> 46.6 us (0.22)
  the two profiles are of different devices: /device:TPU:1 before, /device:TPU:3 now
where the time goes in v2:
time: 46.6 us; the launch traced here: 46.4 us
  Pallas kernels  42.1 us (90%)
  local copies, waits for them, and re-layouts  4.25 us (9%)
    pallas_call x1, Pallas kernels, shards(): pl.pallas_call(kernel, out_shape=jax.ShapeDtypeStruct((2048, 128), F32),...  42.1 us
    unnamed x11, local copies, waits for them, and re-layouts  4.25 us

profile of v2, /device:TPU:3, one launch (start us, length us, event | category | flops | bytes accessed | tf_op | source)
XLA Modules:
  0.0 46.4 jit_solution(16789074425767087558)
XLA Ops:
  0.0 0.0 copy-start.4
  0.0 0.0 copy-start.2
  0.0 0.7 %copy-done.4 = f32[4]{0:T(128)S(1)} copy-done((f32[4]{0:T(128)S(1)}, f32[4]{0:T(128)}, u32[]{:S(2)}) %copy-start.4) | copy-done | bytes 40
  0.7 0.0 copy-done.2
  0.7 0.0 copy-start
  0.7 1.2 %copy-done = f32[1,1,262144]{2,1,0:T(1,128)S(1)} copy-done((f32[1,1,262144]{2,1,0:T(1,128)S(1)}, f32[1,1,262144]{2,1,0:T(1,128)}, u32[]{:S(2)}) %copy-start) | copy-done | bytes 1048600
  1.9 0.0 copy-start.1
  1.9 0.7 %copy-done.1 = f32[2,4,7]{2,1,0:T(4,128)S(1)} copy-done((f32[2,4,7]{2,1,0:T(4,128)S(1)}, f32[2,4,7]{2,1,0:T(4,128)}, u32[]{:S(2)}) %copy-start.1) | copy-done | bytes 248
  2.6 0.0 copy-start.3
  2.6 0.7 %copy-done.3 = s32[2,4]{1,0:T(2,128)S(1)} copy-done((s32[2,4]{1,0:T(2,128)S(1)}, s32[2,4]{1,0:T(2,128)}, u32[]{:S(2)}) %copy-start.3) | copy-done | bytes 56
  3.3 42.1 %layers.1 = f32[2048,128]{1,0:T(8,128)S(1)} custom-call(f32[2048,128]{1,0:T(8,128)S(1)} %bitcast.3, f32[2,4,7]{2,1,0:T(4,128)S(1)} %copy-done.1, s32[2,4]{1,0:T(2,128)S(1)} %copy-done.2, s32[2,4]{1,0:T(2,128)S(1)} %copy-done.3, f32[4]{0:T(128)S(1)} %copy-done.4), custom_call_target="tpu_custom_call" | custom-call | tf_op jit(solution)/shard_map/layers/pallas_call | solution.py:292
  45.4 1.0 %copy.7 = f32[1,1,262144]{2,1,0:T(1,128)} copy(f32[1,1,262144]{2,1,0:T(1,128)S(1)} %bitcast.2) | data formatting | bytes 2097152
Async XLA Ops:
  0.0 0.7 %copy-start.4 = (f32[4]{0:T(128)S(1)}, f32[4]{0:T(128)}, u32[]{:S(2)}) copy-start(f32[4]{0:T(128)} %final.1) | copy-start | bytes 52
  0.0 0.7 %copy-start.2 = (s32[2,4]{1,0:T(2,128)S(1)}, s32[2,4]{1,0:T(2,128)}, u32[]{:S(2)}) copy-start(s32[2,4]{1,0:T(2,128)} %masks.1) | copy-start | bytes 100
  0.7 1.2 %copy-start = (f32[1,1,262144]{2,1,0:T(1,128)S(1)}, f32[1,1,262144]{2,1,0:T(1,128)}, u32[]{:S(2)}) copy-start(f32[1,1,262144]{2,1,0:T(1,128)} %param.5) | copy-start | bytes 3145732
  1.9 0.7 %copy-start.1 = (f32[2,4,7]{2,1,0:T(4,128)S(1)}, f32[2,4,7]{2,1,0:T(4,128)}, u32[]{:S(2)}) copy-start(f32[2,4,7]{2,1,0:T(4,128)} %angles.1) | copy-start | bytes 676
  2.6 0.7 %copy-start.3 = (s32[2,4]{1,0:T(2,128)S(1)}, s32[2,4]{1,0:T(2,128)}, u32[]{:S(2)}) copy-start(s32[2,4]{1,0:T(2,128)} %controls.1) | copy-start | bytes 100

commit v3 on v2

--- a/solution.py
+++ b/solution.py
@@ -10,6 +10,7 @@
 NATURAL = (0, 1, 2, 3, 4, 5, 6)
 MOVED = (6, 3, 4, 5, 0, 1, 2)
 STARTS = (0, 7, 11, 18)
+FAR_FIRST = tuple((dx, dy) for dx in (2, 1, 3, 0) for dy in (2, 1, 3, 0))
 
 
 def iota(shape, dim):
@@ -94,15 +95,22 @@
 
 
 def kernel(
-    x_hbm, angles, masks, controls, final, out_hbm,
-    x_v, mid, send1, recv1, send2, recv2, signs, row_mats, lane_mats,
+    x_hbm, angles_hbm, masks_hbm, controls_hbm, final_hbm, out,
+    x_v, angles, masks, controls, final,
+    mid, send1, recv1, send2, recv2, signs, row_mats, lane_mats,
     in_sem, own_sem, send_sem, recv_sem,
 ):
     qa = lax.axis_index("qa")
     qb = lax.axis_index("qb")
     me = qa * 16 + qb
-    load = pltpu.make_async_copy(x_hbm, x_v, in_sem)
-    load.start()
+    loads = [
+        pltpu.make_async_copy(source, place, in_sem.at[slot])
+        for slot, (source, place) in enumerate((
+            (angles_hbm, angles), (masks_hbm, masks), (controls_hbm, controls),
+            (final_hbm, final), (x_hbm, x_v)))
+    ]
+    for load in loads:
+        load.start()
 
     x, zh = lax.div(qa, 2), lax.rem(qa, 2)
     y, zl, core = lax.div(qb, 4), lax.rem(lax.div(qb, 2), 2), lax.rem(qb, 2)
@@ -127,8 +135,15 @@
             action(x * 32 + y * 4 + other)
 
     barrier = pltpu.get_barrier_semaphore()
-    everyone(lambda target: pl.semaphore_signal(
-        barrier, inc=1, device_id=target, device_id_type=pl.DeviceIdType.LOGICAL))
+    columns = [lax.rem(x + dx, 4) * 32 for dx in range(4)]
+    lines = [lax.rem(y + dy, 4) * 4 for dy in range(4)]
+    for dx, dy in FAR_FIRST:
+        base = columns[dx] + lines[dy]
+        for other in near if (dx, dy) != (0, 0) else near[:7]:
+            pl.semaphore_signal(
+                barrier, inc=1, device_id=base + other, device_id_type=pl.DeviceIdType.LOGICAL)
+    for load in loads[:4]:
+        load.wait()
 
     lane1 = iota((1, 128), 1)
     mask_lanes = jnp.zeros((1, 128), jnp.int32)
@@ -163,36 +178,35 @@
 
     store_row_matrix(row_mats, 0, row_matrix(0, 1, MOVED, NATURAL))
     store_row_matrix(row_mats, 1, row_matrix(0, 2, NATURAL, NATURAL))
-    load.wait()
-
-    spot = row * 128 + iota((128, 128), 1) + me * 262144
-
-    def first_gate(pair, carry):
+    lanes8, sub8 = iota((8, 128), 1), iota((8, 128), 0)
+    column = iota((128, 128), 1)
+    parity = parity_at(0, row * 128 + column + me * 262144)
+    first_signs = jnp.where(parity == 1, -1.0, 1.0)
+    loads[4].wait()
+    for pair in range(8):
         blocks = []
         for i in range(2):
             a = pair * 2 + i
-            value = x_v[pl.ds(pl.multiple_of(a * 128, 128), 128), :]
-            blocks.append(jnp.where(parity_at(0, spot + a * 16384) == 1, -value, value))
-        out = row_gate(row_mats[0], jnp.concatenate(blocks, axis=1))
-        for i in range(2):
-            at = pl.multiple_of((pair * 2 + i) * 8, 8)
-            mid[:, pl.ds(at, 8), :] = out[:, i * 128:(i + 1) * 128].reshape(16, 8, 128)
-        return carry
-
-    lax.fori_loop(0, 8, first_gate, 0)
-
-    def second_gate(pair, carry):
-        kk = pair * 2
-        out = row_gate(row_mats[1], jnp.concatenate([mid[kk], mid[kk + 1]], axis=1))
-        for i in range(2):
-            chunk, group = lax.div(kk + i, 8), lax.rem(kk + i, 8)
-            part = out[:, i * 128:(i + 1) * 128].reshape(16, 8, 128)
-            for a in range(16):
-                send1[chunk, pl.ds(pl.multiple_of((a * 8 + group) * 8, 8), 8), :] = part[a]
-        return carry
-
-    lax.fori_loop(0, 8, second_gate, 0)
-    pl.semaphore_wait(barrier, 127)
+            bits = [((a * 16384) >> controls[0, gate]) & 1 for gate in range(4)]
+            flip = (bits[0] & lanes8) ^ (bits[1] & sub8) ^ (bits[3] & core)
+            even = jnp.where((flip & 1) == 1, -1.0, 1.0)
+            odd = jnp.where(((flip ^ bits[2]) & 1) == 1, -1.0, 1.0)
+            factor = jnp.concatenate([even, even, odd, odd] * 4, axis=0)
+            blocks.append(x_v[a * 128:(a + 1) * 128, :] * first_signs * factor)
+        out_pair = row_gate(row_mats[0], jnp.concatenate(blocks, axis=1))
+        for i in range(2):
+            a = pair * 2 + i
+            mid[:, a * 8:(a + 1) * 8, :] = out_pair[:, i * 128:(i + 1) * 128].reshape(16, 8, 128)
+
+    def second_gate(chunk):
+        for group in range(0, 8, 2):
+            kk = chunk * 8 + group
+            mixed = row_gate(row_mats[1], jnp.concatenate([mid[kk], mid[kk + 1]], axis=1))
+            for i in range(2):
+                part = mixed[:, i * 128:(i + 1) * 128].reshape(16, 8, 128)
+                for a in range(16):
+                    at = (a * 8 + group + i) * 8
+                    send1[chunk, at:at + 8, :] = part[a]
 
     def rows_of(device):
         return pl.ds(pl.multiple_of(device * 8, 8), 8)
@@ -214,7 +228,10 @@
         others = landing.at[chunk, pl.ds(0, 127 * 8)]
         pltpu.make_async_copy(others, others, recv_sem.at[slot]).wait()
 
+    second_gate(0)
+    pl.semaphore_wait(barrier, 127)
     ship(0, 0, send1, recv1)
+    second_gate(1)
     ship(0, 1, send1, recv1)
 
     store_row_matrix(row_mats, 2, row_matrix(0, 3, NATURAL, NATURAL))
@@ -262,46 +279,38 @@
     for chunk in range(2):
         landed(1, chunk, send2, recv2)
 
-    def third_gate(pair, carry):
+    for pair in range(8):
         blocks = []
         for i in range(2):
-            rows = pl.ds(pl.multiple_of((pair * 2 + i) * 64, 64), 64)
-            blocks.append(jnp.concatenate([recv2[0, rows, :], recv2[1, rows, :]], axis=0))
-        out = row_gate(row_mats[4], jnp.concatenate(blocks, axis=1))
-        for i in range(2):
-            at = pl.multiple_of((pair * 2 + i) * 8, 8)
-            mid[:, pl.ds(at, 8), :] = out[:, i * 128:(i + 1) * 128].reshape(16, 8, 128)
-        return carry
-
-    lax.fori_loop(0, 8, third_gate, 0)
+            at = (pair * 2 + i) * 64
+            blocks.append(jnp.concatenate([recv2[0, at:at + 64, :], recv2[1, at:at + 64, :]], axis=0))
+        out_pair = row_gate(row_mats[4], jnp.concatenate(blocks, axis=1))
+        for i in range(2):
+            a = pair * 2 + i
+            mid[:, a * 8:(a + 1) * 8, :] = out_pair[:, i * 128:(i + 1) * 128].reshape(16, 8, 128)
     for kk in range(0, 16, 2):
-        out = row_gate(row_mats[5], jnp.concatenate([mid[kk], mid[kk + 1]], axis=1))
+        mixed = row_gate(row_mats[5], jnp.concatenate([mid[kk], mid[kk + 1]], axis=1))
         for i in range(2):
             k = (kk + i) // 8 + 2 * ((kk + i) % 8)
-            x_v[pl.ds(k, 128, stride=16), :] = out[:, i * 128:(i + 1) * 128]
-    store = pltpu.make_async_copy(x_v, out_hbm, in_sem)
-    store.start()
+            out[pl.ds(k, 128, stride=16), :] = mixed[:, i * 128:(i + 1) * 128]
     for slot in range(4):
         source = (send1, send2)[slot // 2]
         others = source.at[slot % 2, pl.ds(0, 127 * 8)]
         pltpu.make_async_copy(others, others, send_sem.at[slot]).wait()
-    store.wait()
 
 
 def shards(amplitudes, gate_angles, pair_masks, control_qubits, final_angles):
     out = pl.pallas_call(
         kernel,
         out_shape=jax.ShapeDtypeStruct((2048, 128), F32),
-        in_specs=[
-            pl.BlockSpec(memory_space=pl.ANY),
-            pl.BlockSpec(memory_space=pltpu.VMEM),
-            pl.BlockSpec(memory_space=pltpu.SMEM),
-            pl.BlockSpec(memory_space=pltpu.SMEM),
-            pl.BlockSpec(memory_space=pltpu.SMEM),
-        ],
-        out_specs=pl.BlockSpec(memory_space=pl.ANY),
+        in_specs=[pl.BlockSpec(memory_space=pltpu.HBM)] * 5,
+        out_specs=pl.BlockSpec(memory_space=pltpu.VMEM),
         scratch_shapes=[
             pltpu.VMEM((2048, 128), F32),
+            pltpu.VMEM(gate_angles.shape, F32),
+            pltpu.SMEM(pair_masks.shape, jnp.int32),
+            pltpu.SMEM(control_qubits.shape, jnp.int32),
+            pltpu.SMEM(final_angles.shape, F32),
             pltpu.VMEM((16, 128, 128), F32),
             pltpu.VMEM((2, 1024, 128), F32),
             pltpu.VMEM((2, 1024, 128), F32),
@@ -310,7 +319,7 @@
             pltpu.VMEM((16, 128, 128), F32),
             pltpu.VMEM((7, 256, 256), BF16),
             pltpu.VMEM((2, 256, 256), BF16),
-            pltpu.SemaphoreType.DMA,
+            pltpu.SemaphoreType.DMA((5,)),
             pltpu.SemaphoreType.DMA((4,)),
             pltpu.SemaphoreType.DMA((4,)),
             pltpu.SemaphoreType.DMA((4,)),
@@ -318,7 +327,8 @@
         compiler_params=pltpu.CompilerParams(
             collective_id=0, has_side_effects=True, vmem_limit_bytes=24 * 2**20),
         name="layers",
-    )(amplitudes.reshape(2048, 128), gate_angles, pair_masks, control_qubits, final_angles)
+    )(*(pltpu.with_memory_space_constraint(value, pltpu.HBM) for value in (
+        amplitudes.reshape(2048, 128), gate_angles, pair_masks, control_qubits, final_angles)))
     return out.reshape(amplitudes.shape)
 
 

time: 46.6 us -> 39.8 us (0.85)
  the two profiles are of different devices: /device:TPU:3 before, /device:TPU:1 now
where the time goes in v3:
time: 39.8 us; the launch traced here: 39.7 us
  Pallas kernels  38.7 us (97%)
  local copies, waits for them, and re-layouts  0.97 us (2%)
    pallas_call x1, Pallas kernels, shards(): pl.pallas_call(kernel, out_shape=jax.ShapeDtypeStruct((2048, 128), F32),...  38.7 us
    unnamed x1, local copies, waits for them, and re-layouts  0.97 us

profile of v3, /device:TPU:1, one launch (start us, length us, event | category | flops | bytes accessed | tf_op | source)
XLA Modules:
  0.0 39.7 jit_solution(17560636161288914824)
XLA Ops:
  0.0 38.7 %layers.1 = f32[2048,128]{1,0:T(8,128)S(1)} custom-call(f32[2048,128]{1,0:T(8,128)} %bitcast.3, f32[2,4,7]{2,1,0:T(4,128)} %angles_hbm.1, s32[2,4]{1,0:T(2,128)} %masks_hbm.1, s32[2,4]{1,0:T(2,128)} %controls_hbm.1, f32[4]{0:T(128)} %final_hbm.1), custom_call_target="tpu_custom_call" | custom-call | tf_op jit(solution)/shard_map/layers/pallas_call | solution.py:303
  38.8 1.0 %copy.7 = f32[1,1,262144]{2,1,0:T(1,128)} copy(f32[1,1,262144]{2,1,0:T(1,128)S(1)} %bitcast.2) | data formatting | bytes 2097152

commit v4 on v3

--- a/solution.py
+++ b/solution.py
@@ -10,7 +10,10 @@
 NATURAL = (0, 1, 2, 3, 4, 5, 6)
 MOVED = (6, 3, 4, 5, 0, 1, 2)
 STARTS = (0, 7, 11, 18)
-FAR_FIRST = tuple((dx, dy) for dx in (2, 1, 3, 0) for dy in (2, 1, 3, 0))
+STEPS = [(n // 32, n // 8 % 4, n // 2 % 4, n % 2) for n in range(1, 128)]
+def reach(step):
+    return sum(min(part, 4 - part) for part in step[:3])
+ORDER = sorted(STEPS, key=lambda step: (-reach(step), (step[0] * 32 + step[1] * 8 + step[2] * 2 + step[3]) * 53 % 128))
 
 
 def iota(shape, dim):
@@ -115,33 +118,21 @@
     x, zh = lax.div(qa, 2), lax.rem(qa, 2)
     y, zl, core = lax.div(qb, 4), lax.rem(lax.div(qb, 2), 2), lax.rem(qb, 2)
     z = zh * 2 + zl
-    near = []
-    for dz in (2, 1, 3, 0):
-        tz = lax.rem(z + dz, 4)
-        for dc in (1, 0):
-            tc = lax.rem(core + dc, 2)
-            near.append(lax.div(tz, 2) * 16 + lax.rem(tz, 2) * 2 + tc)
+    way = 1 - 2 * core
+    columns = [lax.rem(x + 4 + way * dx, 4) * 32 for dx in range(4)]
+    lines = [lax.rem(y + 4 + way * dy, 4) * 4 for dy in range(4)]
+    levels = [lax.rem(z + 4 + way * dz, 4) for dz in range(4)]
+    cores = [core, 1 - core]
+    inner = [[lax.div(tz, 2) * 16 + lax.rem(tz, 2) * 2 + tc for tc in cores] for tz in levels]
+    outer = [[column + line for line in lines] for column in columns]
 
     def everyone(action):
-        def far(step, carry):
-            base = lax.rem(x + lax.div(step, 4) + 2, 4) * 32 + lax.rem(y + lax.rem(step, 4) + 2, 4) * 4
-            for other in near:
-                action(base + other)
-            return carry
-
-        lax.fori_loop(0, 10, far, 0)
-        lax.fori_loop(11, 16, far, 0)
-        for other in near[:7]:
-            action(x * 32 + y * 4 + other)
+        for dx, dy, dz, dc in ORDER:
+            action(outer[dx][dy] + inner[dz][dc])
 
     barrier = pltpu.get_barrier_semaphore()
-    columns = [lax.rem(x + dx, 4) * 32 for dx in range(4)]
-    lines = [lax.rem(y + dy, 4) * 4 for dy in range(4)]
-    for dx, dy in FAR_FIRST:
-        base = columns[dx] + lines[dy]
-        for other in near if (dx, dy) != (0, 0) else near[:7]:
-            pl.semaphore_signal(
-                barrier, inc=1, device_id=base + other, device_id_type=pl.DeviceIdType.LOGICAL)
+    everyone(lambda target: pl.semaphore_signal(
+        barrier, inc=1, device_id=target, device_id_type=pl.DeviceIdType.LOGICAL))
     for load in loads[:4]:
         load.wait()
 
@@ -176,6 +167,7 @@
             parity = term if parity is None else parity ^ term
         return parity & 1
 
+    store_lane_matrix(lane_mats, 0, lane_matrix(0))
     store_row_matrix(row_mats, 0, row_matrix(0, 1, MOVED, NATURAL))
     store_row_matrix(row_mats, 1, row_matrix(0, 2, NATURAL, NATURAL))
     lanes8, sub8 = iota((8, 128), 1), iota((8, 128), 0)
@@ -193,7 +185,8 @@
             odd = jnp.where(((flip ^ bits[2]) & 1) == 1, -1.0, 1.0)
             factor = jnp.concatenate([even, even, odd, odd] * 4, axis=0)
             blocks.append(x_v[a * 128:(a + 1) * 128, :] * first_signs * factor)
-        out_pair = row_gate(row_mats[0], jnp.concatenate(blocks, axis=1))
+        mixed = lane_gate(lane_mats[0], jnp.concatenate(blocks, axis=0))
+        out_pair = row_gate(row_mats[0], jnp.concatenate([mixed[:128], mixed[128:]], axis=1))
         for i in range(2):
             a = pair * 2 + i
             mid[:, a * 8:(a + 1) * 8, :] = out_pair[:, i * 128:(i + 1) * 128].reshape(16, 8, 128)
@@ -235,7 +228,6 @@
     ship(0, 1, send1, recv1)
 
     store_row_matrix(row_mats, 2, row_matrix(0, 3, NATURAL, NATURAL))
-    store_lane_matrix(lane_mats, 0, lane_matrix(0))
     store_lane_matrix(lane_mats, 1, lane_matrix(1))
     final_half = jnp.zeros((1, 128), F32)
     for j in range(4):
@@ -261,19 +253,21 @@
 
     for chunk in range(2):
         landed(0, chunk, send1, recv1)
+        values = []
         for m in range(0, 8, 2):
             value = jnp.concatenate(
                 [recv1[chunk, pl.ds(m + i, 128, stride=8), :] for i in range(2)], axis=1)
-            value = row_gate(row_mats[2], value)
-            value = jnp.concatenate([value[:, :128], value[:, 128:]], axis=0)
-            value = lane_gate(lane_mats[0], value)
-            block = chunk * 8 + m
-            value = value * jnp.concatenate([signs[block], signs[block + 1]], axis=0)
+            values.append(row_gate(row_mats[2], value))
+        for pair in range(4):
+            value, block = values[pair], chunk * 8 + pair * 2
+            value = jnp.concatenate(
+                [value[:, :128] * signs[block], value[:, 128:] * signs[block + 1]], axis=0)
             value = lane_gate(lane_mats[1], value)
-            value = jnp.concatenate([value[:128], value[128:]], axis=1)
-            value = row_gate(row_mats[3], value)
+            values[pair] = jnp.concatenate([value[:128], value[128:]], axis=1)
+        for pair in range(4):
+            value = row_gate(row_mats[3], values[pair])
             for i in range(2):
-                send2[chunk, pl.ds(m + i, 128, stride=8), :] = value[:, i * 128:(i + 1) * 128]
+                send2[chunk, pl.ds(pair * 2 + i, 128, stride=8), :] = value[:, i * 128:(i + 1) * 128]
         ship(1, chunk, send2, recv2)
 
     for chunk in range(2):

time: 39.8 us -> 37.8 us (0.950)
  Pallas kernels: 38.7 us -> 36.7 us
    pallas_call x1, Pallas kernels: 38.7 us -> 36.7 us  [shards(): pl.pallas_call(kernel, out_shape=jax.ShapeDtypeStruct((2048, 128), F32),...]
where the time goes in v4:
time: 37.8 us; the launch traced here: 37.7 us
  Pallas kernels  36.7 us (97%)
  local copies, waits for them, and re-layouts  0.97 us (3%)
    pallas_call x1, Pallas kernels, shards(): pl.pallas_call(kernel, out_shape=jax.ShapeDtypeStruct((2048, 128), F32),...  36.7 us
    unnamed x1, local copies, waits for them, and re-layouts  0.97 us

profile of v4, /device:TPU:1, one launch (start us, length us, event | category | flops | bytes accessed | tf_op | source)
XLA Modules:
  0.0 37.7 jit_solution(13542693319773925643)
XLA Ops:
  0.0 36.7 %layers.1 = f32[2048,128]{1,0:T(8,128)S(1)} custom-call(f32[2048,128]{1,0:T(8,128)} %bitcast.3, f32[2,4,7]{2,1,0:T(4,128)} %angles_hbm.1, s32[2,4]{1,0:T(2,128)} %masks_hbm.1, s32[2,4]{1,0:T(2,128)} %controls_hbm.1, f32[4]{0:T(128)} %final_hbm.1), custom_call_target="tpu_custom_call" | custom-call | tf_op jit(solution)/shard_map/layers/pallas_call | solution.py:297
  36.7 1.0 %copy.7 = f32[1,1,262144]{2,1,0:T(1,128)} copy(f32[1,1,262144]{2,1,0:T(1,128)S(1)} %bitcast.2) | data formatting | bytes 2097152

commit v5 on v4

--- a/solution.py
+++ b/solution.py
@@ -8,12 +8,33 @@
 F32 = jnp.float32
 BF16 = jnp.bfloat16
 NATURAL = (0, 1, 2, 3, 4, 5, 6)
-MOVED = (6, 3, 4, 5, 0, 1, 2)
+MOVED = (3, 4, 5, 6, 0, 1, 2)
 STARTS = (0, 7, 11, 18)
 STEPS = [(n // 32, n // 8 % 4, n // 2 % 4, n % 2) for n in range(1, 128)]
-def reach(step):
+
+
+def hops(step):
     return sum(min(part, 4 - part) for part in step[:3])
-ORDER = sorted(STEPS, key=lambda step: (-reach(step), (step[0] * 32 + step[1] * 8 + step[2] * 2 + step[3]) * 53 % 128))
+
+
+def spread(step):
+    return (step[0] * 32 + step[1] * 8 + step[2] * 2 + step[3]) * 53 % 128
+
+
+def first_axis(step):
+    return 0 if step[0] else 1 if step[1] else 2
+
+
+def merged(steps):
+    placed = []
+    for kind in range(3):
+        group = [step for step in steps if first_axis(step) == kind]
+        placed += [((n + 0.5) / len(group), step) for n, step in enumerate(group)]
+    return [step for _, step in sorted(placed)]
+
+
+FAR_FIRST = sorted(STEPS, key=lambda step: (-hops(step), spread(step)))
+SENDS = merged(FAR_FIRST)
 
 
 def iota(shape, dim):
@@ -126,13 +147,13 @@
     inner = [[lax.div(tz, 2) * 16 + lax.rem(tz, 2) * 2 + tc for tc in cores] for tz in levels]
     outer = [[column + line for line in lines] for column in columns]
 
-    def everyone(action):
-        for dx, dy, dz, dc in ORDER:
+    def everyone(action, order):
+        for dx, dy, dz, dc in order:
             action(outer[dx][dy] + inner[dz][dc])
 
     barrier = pltpu.get_barrier_semaphore()
     everyone(lambda target: pl.semaphore_signal(
-        barrier, inc=1, device_id=target, device_id_type=pl.DeviceIdType.LOGICAL))
+        barrier, inc=1, device_id=target, device_id_type=pl.DeviceIdType.LOGICAL), FAR_FIRST)
     for load in loads[:4]:
         load.wait()
 
@@ -191,15 +212,14 @@
             a = pair * 2 + i
             mid[:, a * 8:(a + 1) * 8, :] = out_pair[:, i * 128:(i + 1) * 128].reshape(16, 8, 128)
 
-    def second_gate(chunk):
-        for group in range(0, 8, 2):
-            kk = chunk * 8 + group
-            mixed = row_gate(row_mats[1], jnp.concatenate([mid[kk], mid[kk + 1]], axis=1))
-            for i in range(2):
-                part = mixed[:, i * 128:(i + 1) * 128].reshape(16, 8, 128)
-                for a in range(16):
-                    at = (a * 8 + group + i) * 8
-                    send1[chunk, at:at + 8, :] = part[a]
+    for k in range(0, 16, 2):
+        mixed = row_gate(row_mats[1], jnp.concatenate([mid[k], mid[k + 1]], axis=1))
+        for i in range(2):
+            part = mixed[:, i * 128:(i + 1) * 128].reshape(16, 8, 128)
+            for a in range(16):
+                at = ((a // 2) * 16 + k + i) * 8
+                send1[a % 2, at:at + 8, :] = part[a]
+    pl.semaphore_wait(barrier, 127)
 
     def rows_of(device):
         return pl.ds(pl.multiple_of(device * 8, 8), 8)
@@ -212,7 +232,7 @@
         everyone(lambda target: pltpu.make_async_remote_copy(
             source.at[chunk, rows_of(target)], landing.at[chunk, rows_of(me)],
             send_sem.at[slot], recv_sem.at[slot],
-            device_id=target, device_id_type=pl.DeviceIdType.LOGICAL).start())
+            device_id=target, device_id_type=pl.DeviceIdType.LOGICAL).start(), SENDS)
 
     def landed(stage, chunk, source, landing):
         slot = stage * 2 + chunk
@@ -221,10 +241,7 @@
         others = landing.at[chunk, pl.ds(0, 127 * 8)]
         pltpu.make_async_copy(others, others, recv_sem.at[slot]).wait()
 
-    second_gate(0)
-    pl.semaphore_wait(barrier, 127)
     ship(0, 0, send1, recv1)
-    second_gate(1)
     ship(0, 1, send1, recv1)
 
     store_row_matrix(row_mats, 2, row_matrix(0, 3, NATURAL, NATURAL))
@@ -241,11 +258,11 @@
     store_row_matrix(row_mats, 3, row_gate(row_mats[6], jnp.concatenate([top, top], axis=1))[:, :128])
     store_row_matrix(row_mats, 4, row_matrix(1, 1, MOVED, MOVED))
     store_row_matrix(row_mats, 5, row_matrix(1, 2, NATURAL, NATURAL))
-    here = lax.rem(me, 8) * 256 + lax.div(me, 8) * 16384
+    here = lax.rem(me, 16) * 128 + lax.div(me, 16) * 32768
     device_spot = row * 262144 + iota((128, 128), 1) + here
 
     def layer_signs(block, carry):
-        spots = device_spot + (lax.div(block, 8) * 128 + lax.rem(block, 8) * 2048)
+        spots = device_spot + (lax.div(block, 8) * 16384 + lax.rem(block, 8) * 2048)
         signs[block] = jnp.where(parity_at(1, spots) == 1, -1.0, 1.0)
         return carry
 
@@ -272,21 +289,17 @@
 
     for chunk in range(2):
         landed(1, chunk, send2, recv2)
-
-    for pair in range(8):
-        blocks = []
+        for pair in range(4):
+            at = pair * 256
+            blocks = [recv2[chunk, at:at + 128, :], recv2[chunk, at + 128:at + 256, :]]
+            out_pair = row_gate(row_mats[4], jnp.concatenate(blocks, axis=1))
+            for i in range(2):
+                a = (pair * 2 + i) * 2 + chunk
+                mid[:, a * 8:(a + 1) * 8, :] = out_pair[:, i * 128:(i + 1) * 128].reshape(16, 8, 128)
+    for k in range(0, 16, 2):
+        mixed = row_gate(row_mats[5], jnp.concatenate([mid[k], mid[k + 1]], axis=1))
         for i in range(2):
-            at = (pair * 2 + i) * 64
-            blocks.append(jnp.concatenate([recv2[0, at:at + 64, :], recv2[1, at:at + 64, :]], axis=0))
-        out_pair = row_gate(row_mats[4], jnp.concatenate(blocks, axis=1))
-        for i in range(2):
-            a = pair * 2 + i
-            mid[:, a * 8:(a + 1) * 8, :] = out_pair[:, i * 128:(i + 1) * 128].reshape(16, 8, 128)
-    for kk in range(0, 16, 2):
-        mixed = row_gate(row_mats[5], jnp.concatenate([mid[kk], mid[kk + 1]], axis=1))
-        for i in range(2):
-            k = (kk + i) // 8 + 2 * ((kk + i) % 8)
-            out[pl.ds(k, 128, stride=16), :] = mixed[:, i * 128:(i + 1) * 128]
+            out[pl.ds(k + i, 128, stride=16), :] = mixed[:, i * 128:(i + 1) * 128]
     for slot in range(4):
         source = (send1, send2)[slot // 2]
         others = source.at[slot % 2, pl.ds(0, 127 * 8)]

time: 37.8 us -> 37.1 us (0.981)
  Pallas kernels: 36.7 us -> 36.1 us
    pallas_call x1, Pallas kernels: 36.7 us -> 36.1 us  [shards(): pl.pallas_call(kernel, out_shape=jax.ShapeDtypeStruct((2048, 128), F32),...]
where the time goes in v5:
time: 37.1 us; the launch traced here: 37 us
  Pallas kernels  36.1 us (97%)
  local copies, waits for them, and re-layouts  0.97 us (3%)
    pallas_call x1, Pallas kernels, shards(): pl.pallas_call(kernel, out_shape=jax.ShapeDtypeStruct((2048, 128), F32),...  36.1 us
    unnamed x1, local copies, waits for them, and re-layouts  0.97 us

profile of v5, /device:TPU:1, one launch (start us, length us, event | category | flops | bytes accessed | tf_op | source)
XLA Modules:
  0.0 37.0 jit_solution(7744974713623157662)
XLA Ops:
  0.0 36.1 %layers.1 = f32[2048,128]{1,0:T(8,128)S(1)} custom-call(f32[2048,128]{1,0:T(8,128)} %bitcast.3, f32[2,4,7]{2,1,0:T(4,128)} %angles_hbm.1, s32[2,4]{1,0:T(2,128)} %masks_hbm.1, s32[2,4]{1,0:T(2,128)} %controls_hbm.1, f32[4]{0:T(128)} %final_hbm.1), custom_call_target="tpu_custom_call" | custom-call | tf_op jit(solution)/shard_map/layers/pallas_call | solution.py:310
  36.1 1.0 %copy.7 = f32[1,1,262144]{2,1,0:T(1,128)} copy(f32[1,1,262144]{2,1,0:T(1,128)S(1)} %bitcast.2) | data formatting | bytes 2097152

commit v6 on v5

--- a/solution.py
+++ b/solution.py
@@ -10,6 +10,7 @@
 NATURAL = (0, 1, 2, 3, 4, 5, 6)
 MOVED = (3, 4, 5, 6, 0, 1, 2)
 STARTS = (0, 7, 11, 18)
+FIXED = (-1, -2)
 STEPS = [(n // 32, n // 8 % 4, n // 2 % 4, n % 2) for n in range(1, 128)]
 
 
@@ -65,8 +66,13 @@
     lane = iota((1, 128), 1)
     zero, one = [], []
     for j in range(7):
+        low, up = (sine[j], -sine[j]) if flip else (-sine[j], sine[j])
+        if col_places[j] < 0:
+            fixed = col_places[j] == FIXED[1]
+            zero.append(low if fixed else cosine[j])
+            one.append(cosine[j] if fixed else up)
+            continue
         bit = ((lane >> col_places[j]) & 1) == 1
-        low, up = (sine[j], -sine[j]) if flip else (-sine[j], sine[j])
         zero.append(jnp.where(bit, low, cosine[j]))
         one.append(jnp.where(bit, cosine[j], up))
     at = [row_places.index(place) for place in range(7)]
@@ -121,7 +127,7 @@
 def kernel(
     x_hbm, angles_hbm, masks_hbm, controls_hbm, final_hbm, out,
     x_v, angles, masks, controls, final,
-    mid, send1, recv1, send2, recv2, signs, row_mats, lane_mats,
+    mid, send1, recv1, send2, recv2, signs, row_mats, lane_mats, split_mats,
     in_sem, own_sem, send_sem, recv_sem,
 ):
     qa = lax.axis_index("qa")
@@ -257,7 +263,9 @@
     top = row_matrix(1, 3, NATURAL, NATURAL)
     store_row_matrix(row_mats, 3, row_gate(row_mats[6], jnp.concatenate([top, top], axis=1))[:, :128])
     store_row_matrix(row_mats, 4, row_matrix(1, 1, MOVED, MOVED))
-    store_row_matrix(row_mats, 5, row_matrix(1, 2, NATURAL, NATURAL))
+    for chunk in range(2):
+        high, low = halves(row_matrix(1, 2, NATURAL, (0, 1, 2, FIXED[chunk], 3, 4, 5)))
+        split_mats[chunk] = jnp.concatenate([high, low], axis=1)
     here = lax.rem(me, 16) * 128 + lax.div(me, 16) * 32768
     device_spot = row * 262144 + iota((128, 128), 1) + here
 
@@ -294,12 +302,19 @@
             blocks = [recv2[chunk, at:at + 128, :], recv2[chunk, at + 128:at + 256, :]]
             out_pair = row_gate(row_mats[4], jnp.concatenate(blocks, axis=1))
             for i in range(2):
-                a = (pair * 2 + i) * 2 + chunk
-                mid[:, a * 8:(a + 1) * 8, :] = out_pair[:, i * 128:(i + 1) * 128].reshape(16, 8, 128)
-    for k in range(0, 16, 2):
-        mixed = row_gate(row_mats[5], jnp.concatenate([mid[k], mid[k + 1]], axis=1))
-        for i in range(2):
-            out[pl.ds(k + i, 128, stride=16), :] = mixed[:, i * 128:(i + 1) * 128]
+                at = chunk * 64 + (pair * 2 + i) * 8
+                mid[:, at:at + 8, :] = out_pair[:, i * 128:(i + 1) * 128].reshape(16, 8, 128)
+        for k in range(0, 16, 2):
+            rows = slice(chunk * 64, chunk * 64 + 64)
+            high, low = halves(jnp.concatenate([mid[k, rows], mid[k + 1, rows]], axis=1))
+            mixed = jnp.dot(
+                split_mats[chunk], jnp.concatenate([high, low, high, low], axis=0), preferred_element_type=F32)
+            for i in range(2):
+                part = mixed[:, i * 128:(i + 1) * 128]
+                if chunk == 0:
+                    signs[k + i] = part
+                else:
+                    out[pl.ds(k + i, 128, stride=16), :] = signs[k + i] + part
     for slot in range(4):
         source = (send1, send2)[slot // 2]
         others = source.at[slot % 2, pl.ds(0, 127 * 8)]
@@ -326,6 +341,7 @@
             pltpu.VMEM((16, 128, 128), F32),
             pltpu.VMEM((7, 256, 256), BF16),
             pltpu.VMEM((2, 256, 256), BF16),
+            pltpu.VMEM((2, 128, 256), BF16),
             pltpu.SemaphoreType.DMA((5,)),
             pltpu.SemaphoreType.DMA((4,)),
             pltpu.SemaphoreType.DMA((4,)),

time: 37.1 us -> 37.1 us (level)
  no operation moved by 1% of the time
where the time goes in v6:
time: 37.1 us; the launch traced here: 37 us
  Pallas kernels  36 us (97%)
  local copies, waits for them, and re-layouts  0.97 us (3%)
    pallas_call x1, Pallas kernels, shards(): pl.pallas_call(kernel, out_shape=jax.ShapeDtypeStruct((2048, 128), F32),...  36 us
    unnamed x1, local copies, waits for them, and re-layouts  0.97 us

profile of v6, /device:TPU:1, one launch (start us, length us, event | category | flops | bytes accessed | tf_op | source)
XLA Modules:
  0.0 37.0 jit_solution(9759734377039470706)
XLA Ops:
  0.0 36.0 %layers.1 = f32[2048,128]{1,0:T(8,128)S(1)} custom-call(f32[2048,128]{1,0:T(8,128)} %bitcast.3, f32[2,4,7]{2,1,0:T(4,128)} %angles_hbm.1, s32[2,4]{1,0:T(2,128)} %masks_hbm.1, s32[2,4]{1,0:T(2,128)} %controls_hbm.1, f32[4]{0:T(128)} %final_hbm.1), custom_call_target="tpu_custom_call" | custom-call | tf_op jit(solution)/shard_map/layers/pallas_call | solution.py:325
  36.0 1.0 %copy.7 = f32[1,1,262144]{2,1,0:T(1,128)} copy(f32[1,1,262144]{2,1,0:T(1,128)S(1)} %bitcast.2) | data formatting | bytes 2097152

commit v7 on v6

--- a/solution.py
+++ b/solution.py
@@ -111,6 +111,11 @@
     return out[:, :128] + out[:, 128:]
 
 
+def half_gate(left, first, second):
+    high, low = halves(jnp.concatenate([first, second], axis=1))
+    return jnp.dot(left, jnp.concatenate([high, low, high, low], axis=0), preferred_element_type=F32)
+
+
 def store_row_matrix(ref, slot, matrix):
     high, low = halves(matrix)
     ref[slot] = jnp.concatenate(
@@ -125,9 +130,9 @@
 
 
 def kernel(
-    x_hbm, angles_hbm, masks_hbm, controls_hbm, final_hbm, out,
+    x_hbm, angles_hbm, masks_hbm, controls_hbm, final_hbm, mid, signs, split_mats,
     x_v, angles, masks, controls, final,
-    mid, send1, recv1, send2, recv2, signs, row_mats, lane_mats, split_mats,
+    send1, recv1, send2, recv2, row_mats, lane_mats,
     in_sem, own_sem, send_sem, recv_sem,
 ):
     qa = lax.axis_index("qa")
@@ -304,44 +309,54 @@
             for i in range(2):
                 at = chunk * 64 + (pair * 2 + i) * 8
                 mid[:, at:at + 8, :] = out_pair[:, i * 128:(i + 1) * 128].reshape(16, 8, 128)
-        for k in range(0, 16, 2):
-            rows = slice(chunk * 64, chunk * 64 + 64)
-            high, low = halves(jnp.concatenate([mid[k, rows], mid[k + 1, rows]], axis=1))
-            mixed = jnp.dot(
-                split_mats[chunk], jnp.concatenate([high, low, high, low], axis=0), preferred_element_type=F32)
-            for i in range(2):
-                part = mixed[:, i * 128:(i + 1) * 128]
-                if chunk == 0:
-                    signs[k + i] = part
-                else:
-                    out[pl.ds(k + i, 128, stride=16), :] = signs[k + i] + part
+        if chunk == 0:
+            for k in range(0, 16, 2):
+                mixed = half_gate(split_mats[0], mid[k, 0:64], mid[k + 1, 0:64])
+                for i in range(2):
+                    signs[k + i] = mixed[:, i * 128:(i + 1) * 128]
     for slot in range(4):
         source = (send1, send2)[slot // 2]
         others = source.at[slot % 2, pl.ds(0, 127 * 8)]
         pltpu.make_async_copy(others, others, send_sem.at[slot]).wait()
 
 
+def finish(mid, sums, split_mats, out_hbm, rows, out_sem):
+    shaped = rows.reshape(128, 16, 128)
+    copies = []
+    for k in range(0, 16, 2):
+        mixed = half_gate(split_mats[1], mid[k, 64:128], mid[k + 1, 64:128])
+        for i in range(2):
+            rows[pl.ds(k + i, 128, stride=16), :] = sums[k + i] + mixed[:, i * 128:(i + 1) * 128]
+        if k % 8 == 6:
+            part = slice(k - 6, k + 2)
+            copies.append(pltpu.make_async_copy(shaped.at[:, part], out_hbm.at[:, part], out_sem.at[k // 8]))
+            copies[-1].start()
+    for copy in copies:
+        copy.wait()
+
+
 def shards(amplitudes, gate_angles, pair_masks, control_qubits, final_angles):
-    out = pl.pallas_call(
+    parts = pl.pallas_call(
         kernel,
-        out_shape=jax.ShapeDtypeStruct((2048, 128), F32),
+        out_shape=(
+            jax.ShapeDtypeStruct((16, 128, 128), F32),
+            jax.ShapeDtypeStruct((16, 128, 128), F32),
+            jax.ShapeDtypeStruct((2, 128, 256), BF16),
+        ),
         in_specs=[pl.BlockSpec(memory_space=pltpu.HBM)] * 5,
-        out_specs=pl.BlockSpec(memory_space=pltpu.VMEM),
+        out_specs=[pl.BlockSpec(memory_space=pltpu.VMEM)] * 3,
         scratch_shapes=[
             pltpu.VMEM((2048, 128), F32),
             pltpu.VMEM(gate_angles.shape, F32),
             pltpu.SMEM(pair_masks.shape, jnp.int32),
             pltpu.SMEM(control_qubits.shape, jnp.int32),
             pltpu.SMEM(final_angles.shape, F32),
-            pltpu.VMEM((16, 128, 128), F32),
             pltpu.VMEM((2, 1024, 128), F32),
             pltpu.VMEM((2, 1024, 128), F32),
             pltpu.VMEM((2, 1024, 128), F32),
             pltpu.VMEM((2, 1024, 128), F32),
-            pltpu.VMEM((16, 128, 128), F32),
             pltpu.VMEM((7, 256, 256), BF16),
             pltpu.VMEM((2, 256, 256), BF16),
-            pltpu.VMEM((2, 128, 256), BF16),
             pltpu.SemaphoreType.DMA((5,)),
             pltpu.SemaphoreType.DMA((4,)),
             pltpu.SemaphoreType.DMA((4,)),
@@ -352,6 +367,15 @@
         name="layers",
     )(*(pltpu.with_memory_space_constraint(value, pltpu.HBM) for value in (
         amplitudes.reshape(2048, 128), gate_angles, pair_masks, control_qubits, final_angles)))
+    out = pl.pallas_call(
+        finish,
+        out_shape=jax.ShapeDtypeStruct((128, 16, 128), F32),
+        in_specs=[pl.BlockSpec(memory_space=pltpu.VMEM)] * 3,
+        out_specs=pl.BlockSpec(memory_space=pl.ANY),
+        scratch_shapes=[pltpu.VMEM((2048, 128), F32), pltpu.SemaphoreType.DMA((2,))],
+        compiler_params=pltpu.CompilerParams(vmem_limit_bytes=8 * 2**20),
+        name="finish",
+    )(*parts)
     return out.reshape(amplitudes.shape)
 
 

time: 37.1 us -> 36.9 us (level)
  local copies, waits for them, and re-layouts: 0.97 us -> 0 us
  Pallas kernels: 36 us -> 36.8 us
    unnamed x1 -> x0, local copies, waits for them, and re-layouts: 0.97 us -> none
    pallas_call x1 -> x2, Pallas kernels: 36 us -> 36.8 us  [the longest x1 35.5 us: shards(): pl.pallas_call(kernel, out_shape=(jax.ShapeDtypeStruct((16, 128, 128), F3...]
where the time goes in v7:
time: 36.9 us
  Pallas kernels  36.8 us (100%)
    pallas_call x1, Pallas kernels, shards(): pl.pallas_call(kernel, out_shape=(jax.ShapeDtypeStruct((16, 128, 128), F3...  35.5 us
    pallas_call x1, Pallas kernels, shards(): pl.pallas_call(finish, out_shape=jax.ShapeDtypeStruct((128, 16, 128), F32...  1.31 us

profile of v7, /device:TPU:1, one launch (start us, length us, event | category | flops | bytes accessed | tf_op | source)
XLA Modules:
  0.0 36.9 jit_solution(9346904082528318350)
XLA Ops:
  0.0 35.5 %layers.1 = (f32[16,128,128]{2,1,0:T(8,128)S(1)}, f32[16,128,128]{2,1,0:T(8,128)S(1)}, bf16[2,128,256]{2,1,0:T(8,128)(2,1)S(1)}) custom-call(f32[2048,128]{1,0:T(8,128)} %bitcast.2, f32[2,4,7]{2,1,0:T(4,128)} %angles_hbm.1, s32[2,4]{1,0:T(2,128)} %masks_hbm.1, s32[2,4]{1,0:T(2,128)} %controls_hbm.1, f32[4]{0:T(128)} %final_hbm.1), custom_call_target="tpu_custom_call" | custom-call | tf_op jit(solution)/shard_map/layers/pallas_call | solution.py:339
  35.5 1.3 %finish.1 = f32[128,16,128]{2,1,0:T(8,128)} custom-call(f32[16,128,128]{2,1,0:T(8,128)S(1)} %get-tuple-element.8.mid, f32[16,128,128]{2,1,0:T(8,128)S(1)} %get-tuple-element.9.sums, bf16[2,128,256]{2,1,0:T(8,128)(2,1)S(1)} %get-tuple-element.10.split_mats), custom_call_target="tpu_custom_call" | custom-call | tf_op jit(solution)/shard_map/finish/pallas_call | solution.py:370

commit v8 on v7

--- a/solution.py
+++ b/solution.py
@@ -30,7 +30,7 @@
     placed = []
     for kind in range(3):
         group = [step for step in steps if first_axis(step) == kind]
-        placed += [((n + 0.5) / len(group), step) for n, step in enumerate(group)]
+        placed += [((n + 0.5) / len(group) * (0.8, 0.9, 1)[kind], step) for n, step in enumerate(group)]
     return [step for _, step in sorted(placed)]
 
 
@@ -301,6 +301,9 @@
         ship(1, chunk, send2, recv2)
 
     for chunk in range(2):
+        for slot in (0, 1, 2) if chunk == 0 else (3,):
+            others = (send1, send2)[slot // 2].at[slot % 2, pl.ds(0, 127 * 8)]
+            pltpu.make_async_copy(others, others, send_sem.at[slot]).wait()
         landed(1, chunk, send2, recv2)
         for pair in range(4):
             at = pair * 256
@@ -314,10 +317,6 @@
                 mixed = half_gate(split_mats[0], mid[k, 0:64], mid[k + 1, 0:64])
                 for i in range(2):
                     signs[k + i] = mixed[:, i * 128:(i + 1) * 128]
-    for slot in range(4):
-        source = (send1, send2)[slot // 2]
-        others = source.at[slot % 2, pl.ds(0, 127 * 8)]
-        pltpu.make_async_copy(others, others, send_sem.at[slot]).wait()
 
 
 def finish(mid, sums, split_mats, out_hbm, rows, out_sem):

time: 36.9 us -> 37 us (level)
  no operation moved by 1% of the time
where the time goes in v8:
time: 37 us; the launch traced here: 36.9 us
  Pallas kernels  36.9 us (100%)
    pallas_call x1, Pallas kernels, shards(): pl.pallas_call(kernel, out_shape=(jax.ShapeDtypeStruct((16, 128, 128), F3...  35.6 us
    pallas_call x1, Pallas kernels, shards(): pl.pallas_call(finish, out_shape=jax.ShapeDtypeStruct((128, 16, 128), F32...  1.31 us

profile of v8, /device:TPU:1, one launch (start us, length us, event | category | flops | bytes accessed | tf_op | source)
XLA Modules:
  0.0 36.9 jit_solution(12143071833398271912)
XLA Ops:
  0.0 35.6 %layers.1 = (f32[16,128,128]{2,1,0:T(8,128)S(1)}, f32[16,128,128]{2,1,0:T(8,128)S(1)}, bf16[2,128,256]{2,1,0:T(8,128)(2,1)S(1)}) custom-call(f32[2048,128]{1,0:T(8,128)} %bitcast.2, f32[2,4,7]{2,1,0:T(4,128)} %angles_hbm.1, s32[2,4]{1,0:T(2,128)} %masks_hbm.1, s32[2,4]{1,0:T(2,128)} %controls_hbm.1, f32[4]{0:T(128)} %final_hbm.1), custom_call_target="tpu_custom_call" | custom-call | tf_op jit(solution)/shard_map/layers/pallas_call | solution.py:338
  35.6 1.3 %finish.1 = f32[128,16,128]{2,1,0:T(8,128)} custom-call(f32[16,128,128]{2,1,0:T(8,128)S(1)} %get-tuple-element.8.mid, f32[16,128,128]{2,1,0:T(8,128)S(1)} %get-tuple-element.9.sums, bf16[2,128,256]{2,1,0:T(8,128)(2,1)S(1)} %get-tuple-element.10.split_mats), custom_call_target="tpu_custom_call" | custom-call | tf_op jit(solution)/shard_map/finish/pallas_call | solution.py:369
